TPU v7x, 32 devices: a whole 2x2x4 slice. The times are simulated.
32 devices in a mesh: frame: 16 (over z, x, core), patch: 2 (over y).
Axes of the slice: x: 2, y: 2, z: 4, core: 2. Of those that a mesh axis runs over, the one named last changes fastest.
Arguments:
- clip: bfloat16 [4, 16, 256, 1280], P(None, 'frame', 'patch'), may hold values from -54 to 54
- norm_time: float32 [1280], replicated, may hold values from 0.1 to 1.9
- w_time_qkv: bfloat16 [1280, 1920], replicated, may hold values from -0.15625 to 0.15625
- q_gain_time: float32 [640], replicated, may hold values from 1 to 2
- k_gain_time: float32 [640], replicated, may hold values from 1 to 2
- w_time_out: bfloat16 [640, 1280], replicated, may hold values from -0.25 to 0.25
- norm_space: float32 [1280], replicated, may hold values from 0.1 to 1.9
- w_space_qkv: bfloat16 [1280, 1920], replicated, may hold values from -0.15625 to 0.15625
- q_gain_space: float32 [640], replicated, may hold values from 1 to 2
- k_gain_space: float32 [640], replicated, may hold values from 1 to 2
Outputs:
- spatial_out: bfloat16 [4, 16, 256, 640], P(None, 'frame', 'patch')
All inputs are finite; a program needn't handle non-finite values.
Results may differ from a plain program's by a relative error of at most 0.025.
Values may be sent and summed in bfloat16 or wider, within the bound.
No kernel may reach another device: no remote copies, remote signals or barrier semaphores. Data moves between devices by JAX's collectives and lax.ppermute only.
A program may use at most 128 MiB of HBM per device.

v0:
```python
import jax
import jax.numpy as jnp
from jax import lax
from jax.sharding import PartitionSpec as P

HDIM = 80


epsilon = 1e-06


def layer_norm(token_rows, norm_gain):
    values = token_rows.astype(jnp.float32)
    average = jnp.mean(values, axis=-1, keepdims=True)
    centred = values - average
    variance = jnp.mean(centred * centred, axis=-1, keepdims=True)
    return (centred * lax.rsqrt(variance + epsilon) * norm_gain).astype(jnp.bfloat16)


def head_norm(projected, head_gain, head_size):
    leading = projected.shape[:-1]
    split_heads = projected.reshape(leading + (projected.shape[-1] // head_size, head_size))
    squares = jnp.mean(split_heads * split_heads, axis=-1, keepdims=True)
    scaled = split_heads * lax.rsqrt(squares + epsilon)
    return (scaled.reshape(projected.shape) * head_gain).astype(jnp.bfloat16)


def project_heads(normed, weight, query_gain, key_gain, head_size):
    inner_width = weight.shape[1] // 3
    product = jnp.dot(normed, weight, preferred_element_type=jnp.float32)
    query = head_norm(product[:, :inner_width], query_gain, head_size)
    keys = head_norm(product[:, inner_width : 2 * inner_width], key_gain, head_size)
    values = product[:, 2 * inner_width :].astype(jnp.bfloat16)
    return (query, keys, values)


def frame_attention(query, keys, values):
    clip_count, frame_count, patch_count, inner_width = query.shape
    split = (clip_count, frame_count, patch_count, inner_width // HDIM, HDIM)
    scores = jnp.einsum(
        "cfphd,cgphd->cphfg",
        query.reshape(split),
        keys.reshape(split),
        preferred_element_type=jnp.float32,
    ) * HDIM ** (-0.5)
    exponent = jnp.exp(scores)
    totals = jnp.sum(exponent, axis=-1)
    summed = jnp.einsum(
        "cphfg,cgphd->cfphd",
        exponent.astype(jnp.bfloat16),
        values.reshape(split),
        preferred_element_type=jnp.float32,
    )
    result = summed / jnp.transpose(totals, (0, 3, 1, 2))[..., None]
    result = result.reshape(query.shape).astype(jnp.bfloat16)
    return lax.all_to_all(result, "frame", split_axis=1, concat_axis=2, tiled=True)


def space_start(query):
    clip_count = query.shape[0]
    row_count = query.shape[2]
    head_count = query.shape[3] // HDIM
    query_heads = query.reshape(clip_count, row_count, head_count, HDIM)
    empty = (
        jnp.zeros((clip_count, head_count, row_count), jnp.float32),
        jnp.zeros((clip_count, row_count, head_count, HDIM), jnp.float32),
    )
    return (query_heads, empty)


def space_add(query_heads, keys, values):
    split = (keys.shape[0], keys.shape[2], query_heads.shape[2], HDIM)
    scores = jnp.einsum(
        "cqhd,ckhd->chqk", query_heads, keys.reshape(split), preferred_element_type=jnp.float32
    ) * HDIM ** (-0.5)
    exponent = jnp.exp(scores)
    totals = jnp.sum(exponent, axis=-1)
    summed = jnp.einsum(
        "chqk,ckhd->cqhd",
        exponent.astype(jnp.bfloat16),
        values.reshape(split),
        preferred_element_type=jnp.float32,
    )
    return (totals, summed)


def space_finish(totals, summed):
    result = summed / jnp.transpose(totals, (0, 2, 1))[..., None]
    return result.reshape(
        summed.shape[0], 1, summed.shape[1], summed.shape[2] * summed.shape[3]
    ).astype(jnp.bfloat16)


def body(
    clip,
    norm_time,
    w_time_qkv,
    q_gain_time,
    k_gain_time,
    w_time_out,
    norm_space,
    w_space_qkv,
    q_gain_space,
    k_gain_space,
):
    clip_count, frame_count, pat_count, features = clip.shape
    inner_width = w_time_out.shape[0]
    token_rows = clip.reshape(-1, features)
    normed = layer_norm(token_rows, norm_time)
    local_shape = (clip_count, frame_count, pat_count, inner_width)
    query, keys, values = project_heads(normed, w_time_qkv, q_gain_time, k_gain_time, HDIM)
    pieces = (
        lax.all_to_all(
            query.reshape(local_shape), "frame", split_axis=2, concat_axis=1, tiled=True
        ),
        lax.all_to_all(keys.reshape(local_shape), "frame", split_axis=2, concat_axis=1, tiled=True),
        lax.all_to_all(
            values.reshape(local_shape), "frame", split_axis=2, concat_axis=1, tiled=True
        ),
    )
    attended = frame_attention(pieces[0], pieces[1], pieces[2])
    delta = jnp.dot(
        attended.reshape(-1, inner_width), w_time_out, preferred_element_type=jnp.float32
    )
    mixed = (token_rows.astype(jnp.float32) + delta).astype(jnp.bfloat16)
    space_normed = layer_norm(mixed, norm_space)
    space_query, space_keys, space_values = project_heads(
        space_normed, w_space_qkv, q_gain_space, k_gain_space, HDIM
    )
    space_query = space_query.reshape(local_shape)
    space_keys = space_keys.reshape(local_shape)
    space_values = space_values.reshape(local_shape)
    query_heads, empty = space_start(space_query)
    pieces = (
        lax.all_gather(space_keys, "patch", axis=2, tiled=True),
        lax.all_gather(space_values, "patch", axis=2, tiled=True),
    )
    totals, summed = space_add(query_heads, pieces[0], pieces[1])
    spatial = space_finish(totals, summed)
    return spatial


def solution(mesh):
    in_specs = (P(None, "frame", "patch", None), P(), P(), P(), P(), P(), P(), P(), P(), P())
    out_specs = P(None, "frame", "patch", None)
    return jax.shard_map(body, mesh=mesh, in_specs=in_specs, out_specs=out_specs, check_vma=False)
```

profile of v0, /device:TPU:0, one launch (start us, length us, event | category | flops | bytes accessed | tf_op | source)
XLA Modules:
  0.0 221.6 jit_solution(3652734777082857897)
XLA Ops:
  6.5 1.7 convert_reduce_fusion.1
  9.3 4.9 %fusion.38 = f32[512,1920]{1,0:T(8,128)S(1)} fusion(bf16[512,1280]{1,0:T(8,128)(2,1)S(1)} %fusion.10, bf16[1280,1920]{1,0:T(8,128)(2,1)} %param.12), kind=kOutput, calls=%fused_computation.59 | convolution fusion | flops 2516582400 | bytes 10158080 | tf_op jit(solution)/shard_map/dot_general | solution.py:30
  14.3 1.8 slice_multiply_fusion.3
  16.1 0.9 copy-done.3
  17.0 2.8 %copy.61 = f32[512,640]{0,1:T(8,128)} copy(f32[512,640]{1,0:T(8,128)} %get-tuple-element.11) | data formatting | bytes 2621440 | tf_op jit(solution)/shard_map/mul | solution.py:23
  19.7 1.5 reduce_sum.92
  21.2 1.2 mul.158
  22.4 2.8 %copy.62 = f32[512,640]{1,0:T(8,128)} copy(f32[512,640]{0,1:T(8,128)} %bitcast.60) | data formatting | bytes 2621440 | tf_op jit(solution)/shard_map/mul | solution.py:24
  25.3 2.8 %copy.65 = f32[512,640]{0,1:T(8,128)} copy(f32[512,640]{1,0:T(8,128)} %get-tuple-element.12) | data formatting | bytes 2621440 | tf_op jit(solution)/shard_map/mul | solution.py:23
  28.1 1.5 reduce_sum.93
  29.5 1.2 mul.165
  30.8 2.8 %copy.66 = f32[512,640]{1,0:T(8,128)} copy(f32[512,640]{0,1:T(8,128)} %bitcast.62) | data formatting | bytes 2621440 | tf_op jit(solution)/shard_map/mul | solution.py:24
  33.6 3.6 %multiply_convert_fusion.3 = (bf16[512,640]{1,0:T(8,128)(2,1)}, bf16[512,640]{1,0:T(8,128)(2,1)S(1)}) fusion(f32[512,640]{1,0:T(8,128)} %copy.62, f32[512,1920]{1,0:T(8,128)} %copy-done.3, f32[640]{0:T(1024)S(1)} %copy-done.7, f32[640]{0:T(1024)S(1)} %copy-done.8, f32[512,640]{1,0:T(8,128)} %copy.66), kind=kLoop, calls=%fused_computation.36 | loop fusion | flops 1966080 | bytes 6558720 | tf_op jit(solution)/shard_map/convert_element_type | solution.py:25
  37.2 1.4 copy.67
  38.6 7.4 %all-to-all-start.2 = ((bf16[4,1,128,640]{3,0,1,2:T(4,128)(2,1)}), bf16[4,1,128,640]{3,0,1,2:T(4,128)(2,1)}, u32[]{:S(2)}, u32[]{:S(2)}) async-start(bf16[4,1,128,640]{3,0,1,2:T(4,128)(2,1)} %copy.67), calls=%async_computation.2 | async-start | bytes 1310720 | tf_op jit(solution)/shard_map/all_to_all | solution.py:116
  46.0 2.4 %copy.63 = bf16[4,1,128,640]{3,0,1,2:T(4,128)(2,1)} copy(bf16[4,1,128,640]{3,2,0,1:T(8,128)(2,1)} %bitcast.68) | data formatting | bytes 1310720 | tf_op jit(solution)/shard_map/reshape | solution.py:114
  48.4 14.2 %all-to-all-done.2 = bf16[4,1,128,640]{3,0,1,2:T(4,128)(2,1)} async-done(((bf16[4,1,128,640]{3,0,1,2:T(4,128)(2,1)}), bf16[4,1,128,640]{3,0,1,2:T(4,128)(2,1)}, u32[]{:S(2)}, u32[]{:S(2)}) %all-to-all-start.2) | async-done | bytes 655392 | tf_op jit(solution)/shard_map/all_to_all | solution.py:116
  62.7 4.8 %all-to-all-start.1 = ((bf16[4,1,128,640]{3,0,1,2:T(4,128)(2,1)}), bf16[4,1,128,640]{3,0,1,2:T(4,128)(2,1)}, u32[]{:S(2)}, u32[]{:S(2)}) async-start(bf16[4,1,128,640]{3,0,1,2:T(4,128)(2,1)} %copy.63), calls=%async_computation.1 | async-start | bytes 1310720 | tf_op jit(solution)/shard_map/all_to_all | solution.py:113
  67.5 1.4 slice.43
  68.9 1.3 copy.59
  70.2 13.9 %all-to-all-done.1 = bf16[4,1,128,640]{3,0,1,2:T(4,128)(2,1)} async-done(((bf16[4,1,128,640]{3,0,1,2:T(4,128)(2,1)}), bf16[4,1,128,640]{3,0,1,2:T(4,128)(2,1)}, u32[]{:S(2)}, u32[]{:S(2)}) %all-to-all-start.1) | async-done | bytes 655392 | tf_op jit(solution)/shard_map/all_to_all | solution.py:113
  84.2 4.8 %all-to-all-start = ((bf16[4,1,128,640]{3,0,1,2:T(4,128)(2,1)}), bf16[4,1,128,640]{3,0,1,2:T(4,128)(2,1)}, u32[]{:S(2)}, u32[]{:S(2)}) async-start(bf16[4,1,128,640]{3,0,1,2:T(4,128)(2,1)} %copy.59), calls=%async_computation | async-start | bytes 1310720 | tf_op jit(solution)/shard_map/all_to_all | solution.py:117
  89.2 3.0 %reshape.187 = bf16[4,16,8,8,80]{4,3,0,2,1:T(8,128)(2,1)} reshape(bf16[4,1,128,640]{3,0,1,2:T(4,128)(2,1)} %all-to-all-done.1) | data formatting | bytes 1310720 | tf_op jit(solution)/shard_map/reshape | solution.py:42
  92.2 3.0 %reshape.188 = bf16[4,16,8,8,80]{4,3,0,2,1:T(8,128)(2,1)} reshape(bf16[4,1,128,640]{3,0,1,2:T(4,128)(2,1)} %all-to-all-done.2) | data formatting | bytes 1310720 | tf_op jit(solution)/shard_map/reshape | solution.py:43
  95.2 4.6 %fusion.15 = (f32[4,8,8,16]{3,2,1,0:T(8,128)S(1)}, f32[4,8,8,16,16]{3,4,2,1,0:T(8,128)}) fusion(bf16[4,16,8,8,80]{4,3,0,2,1:T(8,128)(2,1)} %reshape.188, bf16[4,16,8,8,80]{4,3,0,2,1:T(8,128)(2,1)} %reshape.187), kind=kOutput, calls=%fused_computation.23 | convolution fusion | flops 10612736 | bytes 1589248 | tf_op jit(solution)/shard_map/cfphd,cgphd->cphfg/dot_general | solution.py:40
  99.8 5.9 %all-to-all-done = bf16[4,1,128,640]{3,0,1,2:T(4,128)(2,1)} async-done(((bf16[4,1,128,640]{3,0,1,2:T(4,128)(2,1)}), bf16[4,1,128,640]{3,0,1,2:T(4,128)(2,1)}, u32[]{:S(2)}, u32[]{:S(2)}) %all-to-all-start) | async-done | bytes 655392 | tf_op jit(solution)/shard_map/all_to_all | solution.py:117
  105.6 3.0 %reshape.186 = bf16[4,16,8,8,80]{4,3,0,2,1:T(8,128)(2,1)} reshape(bf16[4,1,128,640]{3,0,1,2:T(4,128)(2,1)} %all-to-all-done) | data formatting | bytes 1310720 | tf_op jit(solution)/shard_map/reshape | solution.py:51
  108.6 3.4 %fusion.13 = bf16[4,16,8,8,80]{4,1,3,2,0:T(8,128)(2,1)S(1)} fusion(f32[4,8,8,16,16]{3,4,2,1,0:T(8,128)} %get-tuple-element.16, bf16[4,16,8,8,80]{4,3,0,2,1:T(8,128)(2,1)} %reshape.186, f32[4,16,8,8]{1,3,2,0:T(8,128)S(1)} %bitcast.75), kind=kOutput, calls=%fused_computation.19 | convolution fusion | flops 11272192 | bytes 1589248 | tf_op jit(solution)/shard_map/cphfg,cgphd->cfphd/dot_general | solution.py:48
  112.0 1.2 copy.92
  113.3 2.7 %reshape.189 = bf16[4,16,8,640]{3,2,0,1:T(8,128)(2,1)} reshape(bf16[4,16,8,8,80]{4,3,2,0,1:T(8,128)(2,1)} %copy.92) | data formatting | bytes 1310720 | tf_op jit(solution)/shard_map/convert_element_type | solution.py:55
  115.9 23.0 %all_to_all.16 = bf16[4,16,8,640]{3,2,0,1:T(8,128)(2,1)S(1)} all-to-all(bf16[4,16,8,640]{3,2,0,1:T(8,128)(2,1)} %reshape.189), channel_id=1, replica_groups=mesh['frame'=16,'patch'=2] {'frame'}, dimensions={1} | all-to-all | bytes 1310720 | tf_op jit(solution)/shard_map/all_to_all | solution.py:56
  139.0 1.3 convert_reduce_fusion
  141.0 5.0 %fusion.20 = f32[512,1920]{1,0:T(8,128)S(1)} fusion(bf16[1280,1920]{1,0:T(8,128)(2,1)} %param.17, bf16[512,1280]{1,0:T(8,128)(2,1)S(1)} %get-tuple-element.18, f32[1280]{0:T(1024)S(1)} %copy-done.11, f32[512]{0:T(512)S(1)} %add_rsqrt_fusion.4, f32[512]{0:T(512)S(1)} %broadcast_multiply_fusion), kind=kOutput, calls=%fused_computation.26 | convolution fusion | flops 2519859200 | bytes 10167296 | tf_op jit(solution)/shard_map/dot_general | solution.py:30
  146.2 1.7 copy-done.4
  147.9 1.5 copy.77
  149.4 1.5 reduce_sum.97
  151.0 1.5 copy.78
  153.3 1.5 copy.81
  154.8 3.2 %multiply_convert_fusion.1 = (bf16[512,640]{1,0:T(8,128)(2,1)S(1)}, bf16[512,640]{1,0:T(8,128)(2,1)}) fusion(f32[512,640]{1,0:T(8,128)S(1)} %copy-done.5, f32[512,1920]{1,0:T(8,128)} %copy-done.4, f32[640]{0:T(1024)S(1)} %copy-done.9, f32[640]{0:T(1024)S(1)} %copy-done.10, f32[512,640]{1,0:T(8,128)} %copy.81), kind=kLoop, calls=%fused_computation.31 | loop fusion | flops 1966080 | bytes 6558720 | tf_op jit(solution)/shard_map/convert_element_type | solution.py:25
  158.1 2.2 %slice.42 = bf16[512,640]{1,0:T(8,128)(2,1)} slice(f32[512,1920]{1,0:T(8,128)} %copy-done.4), slice={[0:512], [1280:1920]} | slice | bytes 1310720 | tf_op jit(solution)/shard_map/slice | solution.py:33
  160.4 1.0 reshape.190
  161.4 19.7 %all-gather.5.cloned.1.call-done = bf16[4,1,256,640]{3,2,0,1:T(8,128)(2,1)} async-done(((bf16[4,1,128,640]{3,2,0,1:T(8,128)(2,1)}), bf16[4,1,256,640]{3,2,0,1:T(8,128)(2,1)}) %all-gather.5.cloned.1.call-update) | async-done | bytes 1310736 | tf_op jit(solution)/shard_map/all_gather | solution.py:135
  181.1 1.6 copy.82
  182.7 2.8 %fusion = (f32[4,8,128]{2,1,0:T(8,128)S(1)}, f32[4,8,128,256]{3,2,1,0:T(8,128)}) fusion(bf16[4,256,8,80]{1,3,2,0:T(8,128)(2,1)S(1)} %bitcast.66, bf16[4,128,8,80]{3,2,1,0:T(8,128)(2,1)S(1)} %reshape.190), kind=kOutput, calls=%fused_computation.1 | convolution fusion | flops 169865216 | bytes 6176768 | tf_op jit(solution)/shard_map/cqhd,ckhd->chqk/dot_general | solution.py:73
  185.5 21.4 %all-gather.3.cloned.1.call-done = bf16[4,1,256,640]{3,2,0,1:T(8,128)(2,1)} async-done(((bf16[4,1,128,640]{3,2,0,1:T(8,128)(2,1)}), bf16[4,1,256,640]{3,2,0,1:T(8,128)(2,1)}) %all-gather.3.cloned.1.call-update) | async-done | bytes 1310736 | tf_op jit(solution)/shard_map/all_gather | solution.py:136
  206.9 1.6 copy.76
  208.6 4.0 %divide_convert_fusion = bf16[4,128,8,80]{1,3,2,0:T(8,128)(2,1)} fusion(bf16[4,256,8,80]{1,3,2,0:T(8,128)(2,1)S(1)} %bitcast.72, f32[4,8,128,256]{3,2,1,0:T(8,128)} %get-tuple-element.20, f32[4,128,8]{1,2,0:T(8,128)S(1)} %bitcast.76), kind=kOutput, calls=%fused_computation.29 | convolution fusion | flops 170524672 | bytes 6176768 | tf_op jit(solution)/shard_map/chqk,ckhd->cqhd/dot_general | solution.py:78
  212.6 2.2 copy.84
  (43 shorter events, 3.2 us)
Async XLA Ops:
  6.5 132.5 %copy-start = (bf16[640,1280]{1,0:T(8,128)(2,1)S(1)}, bf16[640,1280]{1,0:T(8,128)(2,1)}, u32[]{:S(2)}) copy-start(bf16[640,1280]{1,0:T(8,128)(2,1)} %param.15) | copy-start | bytes 4915204
  6.5 1.8 copy-start.2
  6.5 2.3 %copy-start.6 = (f32[1280]{0:T(1024)S(1)}, f32[1280]{0:T(1024)}, u32[]{:S(2)}) copy-start(f32[1280]{0:T(1024)} %param.11) | copy-start | bytes 15364
  14.3 2.7 %copy-start.3 = (f32[512,1920]{1,0:T(8,128)}, f32[512,1920]{1,0:T(8,128)S(1)}, u32[]{:S(2)}) copy-start(f32[512,1920]{1,0:T(8,128)S(1)} %fusion.38) | copy-start | bytes 11796484
  30.8 2.8 %copy-start.7 = (f32[640]{0:T(1024)S(1)}, f32[640]{0:T(1024)}, u32[]{:S(2)}) copy-start(f32[640]{0:T(1024)} %param.13) | copy-start | bytes 7684
  30.8 2.8 %copy-start.8 = (f32[640]{0:T(1024)S(1)}, f32[640]{0:T(1024)}, u32[]{:S(2)}) copy-start(f32[640]{0:T(1024)} %param.14) | copy-start | bytes 7684
  38.6 24.1 %all-to-all-start.2 = ((bf16[4,1,128,640]{3,0,1,2:T(4,128)(2,1)}), bf16[4,1,128,640]{3,0,1,2:T(4,128)(2,1)}, u32[]{:S(2)}, u32[]{:S(2)}) async-start(bf16[4,1,128,640]{3,0,1,2:T(4,128)(2,1)} %copy.67), calls=%async_computation.2 | async-start | bytes 1310720 | tf_op jit(solution)/shard_map/all_to_all | solution.py:116
  62.7 21.5 %all-to-all-start.1 = ((bf16[4,1,128,640]{3,0,1,2:T(4,128)(2,1)}), bf16[4,1,128,640]{3,0,1,2:T(4,128)(2,1)}, u32[]{:S(2)}, u32[]{:S(2)}) async-start(bf16[4,1,128,640]{3,0,1,2:T(4,128)(2,1)} %copy.63), calls=%async_computation.1 | async-start | bytes 1310720 | tf_op jit(solution)/shard_map/all_to_all | solution.py:113
  84.2 21.5 %all-to-all-start = ((bf16[4,1,128,640]{3,0,1,2:T(4,128)(2,1)}), bf16[4,1,128,640]{3,0,1,2:T(4,128)(2,1)}, u32[]{:S(2)}, u32[]{:S(2)}) async-start(bf16[4,1,128,640]{3,0,1,2:T(4,128)(2,1)} %copy.59), calls=%async_computation | async-start | bytes 1310720 | tf_op jit(solution)/shard_map/all_to_all | solution.py:117
  89.0 92.1 %all-gather.5.cloned.1.call-start = ((), (), s32[]{:S(2)}) async-start(), calls=%async_computation.5 | async-start | bytes 1966080 | tf_op jit(solution)/shard_map/all_gather | solution.py:135
  140.3 0.7 copy-start.11
  146.1 1.9 copy-start.4
  153.3 1.5 copy-start.5
  153.3 1.5 copy-start.9
  153.3 1.5 copy-start.10
  158.1 48.9 %all-gather.3.cloned.1.call-start = ((), (), s32[]{:S(2)}) async-start(), calls=%async_computation.4 | async-start | bytes 1966080 | tf_op jit(solution)/shard_map/all_gather | solution.py:136
  208.5 6.2 %copy-start.1 = (bf16[640,1280]{1,0:T(8,128)(2,1)S(1)}, bf16[640,1280]{1,0:T(8,128)(2,1)}, u32[]{:S(2)}) copy-start(bf16[640,1280]{1,0:T(8,128)(2,1)} %param.15) | copy-start | bytes 4915204
Sparse Core Ops, SparseCore 0:
  158.2 22.8 all-gather.4
  182.7 24.2 all-gather.2
where the time goes:
time: 223 us; the launch traced here: 222 us
  waiting for transfers between devices  75.2 us (34%)
  local copies, waits for them, and re-layouts  49.8 us (22%)
  matrix products  26 us (12%)
  blocking collectives  23 us (10%)
  starting transfers between devices  17.3 us (8%)
  other arithmetic  16.6 us (7%)
  between operations  13.7 us (6%)
    all_to_all x1, blocking collectives, frame_attention(): lax.all_to_all(result, 'frame', split_axis=1, concat_axis=2, tiled=True)  23 us
    all_gather x1, waiting for transfers between devices, body(): lax.all_gather(space_values, 'patch', axis=2, tiled=True)  21.4 us
    all_gather x1, waiting for transfers between devices, body(): lax.all_gather(space_keys, 'patch', axis=2, tiled=True)  19.7 us
    all_to_all x1, waiting for transfers between devices, body(): lax.all_to_all(keys.reshape(local_shape), 'frame', split_axis=2, concat_a...  14.2 us
    all_to_all x1, waiting for transfers between devices, body(): lax.all_to_all(query.reshape(local_shape), 'frame', split_axis=2, concat_...  13.9 us
    mul x8, local copies, waits for them, and re-layouts, head_norm(): scaled = split_heads * lax.rsqrt(squares + epsilon)  11.4 us
    dot_general x2, matrix products, project_heads(): product = jnp.dot(normed, weight, preferred_element_type=jnp.float32)  9.98 us
    mul x4, local copies, waits for them, and re-layouts, head_norm(): squares = jnp.mean(split_heads * split_heads, axis=-1, keepdims=True)  7.42 us
  transfers between devices with their start and end apart: 5, of which 5 were waited for; matrix products, arithmetic and copies ran while one was open for 11% of the time, Pallas kernels for 0%

commit v1 on v0

v1 whole, which is shorter than its diff:
```python
import functools

import jax
import jax.numpy as jnp
from jax import lax
from jax.experimental import pallas as pl
from jax.experimental.pallas import tpu as pltpu
from jax.sharding import PartitionSpec as P

HDIM = 80
LANES = 128
EPS = 1e-06
CELLS = 16
MIB = 1024 * 1024

VMEM = pl.BlockSpec(memory_space=pltpu.VMEM)
ANY = pl.BlockSpec(memory_space=pl.ANY)


def layer_norm(values, norm_gain):
    average = jnp.mean(values, axis=-1, keepdims=True)
    centred = values - average
    variance = jnp.mean(centred * centred, axis=-1, keepdims=True)
    return (centred * lax.rsqrt(variance + EPS) * norm_gain).astype(jnp.bfloat16)


def head_norm(part, gain, ones):
    sums = jnp.dot((part * part).astype(jnp.bfloat16), ones, preferred_element_type=jnp.float32)
    return (part * lax.rsqrt(sums * (1.0 / HDIM) + EPS) * gain).astype(jnp.bfloat16)


def lanes_of(head, tile, rows):
    lane = lax.broadcasted_iota(jnp.int32, (rows, LANES), 1) + tile * LANES
    return (lane >= head * HDIM) & (lane < (head + 1) * HDIM)


def attend(query, load_keys, load_values, inner, keep):
    rows = query.shape[0]
    tiles = [None] * (inner // LANES)
    for head in range(inner // HDIM):
        first, last = head * HDIM // LANES, ((head + 1) * HDIM - 1) // LANES
        lo, hi = first * LANES, (last + 1) * LANES
        masks = [lanes_of(head, tile, rows) for tile in range(first, last + 1)]
        own = jnp.concatenate(
            [
                jnp.where(mask, query[:, t * LANES : (t + 1) * LANES], jnp.zeros((), query.dtype))
                for mask, t in zip(masks, range(first, last + 1))
            ],
            axis=1,
        )
        scores = lax.dot_general(
            own, load_keys(lo, hi), (((1,), (1,)), ((), ())), preferred_element_type=jnp.float32
        )
        exponent = jnp.exp(scores * HDIM ** (-0.5))
        if keep is not None:
            exponent = jnp.where(keep, exponent, 0.0)
        total = jnp.sum(exponent, axis=-1, keepdims=True)
        summed = jnp.dot(
            exponent.astype(jnp.bfloat16), load_values(lo, hi), preferred_element_type=jnp.float32
        )
        result = summed * (1.0 / total)
        for i, t in enumerate(range(first, last + 1)):
            piece = result[:, i * LANES : (i + 1) * LANES]
            tiles[t] = piece if tiles[t] is None else jnp.where(masks[i], piece, tiles[t])
    return jnp.concatenate(tiles, axis=1)


def partner_rows(k, cells):
    chip = lax.axis_index("frame") // 2
    return pl.ds(pl.multiple_of((chip ^ k) * cells, cells), cells)


def pack_kernel(cells, x_ref, *out_refs):
    for k, out_ref in enumerate(out_refs):
        out_ref[...] = x_ref[partner_rows(k, cells), :]


def time_kernel(count, *refs):
    pieces, weights, (q_ref, kv_ref) = refs[:count], refs[count : count + 5], refs[-2:]
    norm_ref, w_ref, qg_ref, kg_ref, ones_ref = weights
    inner = w_ref.shape[1] // 3
    normed = jnp.concatenate(
        [layer_norm(ref[...].astype(jnp.float32), norm_ref[...]) for ref in pieces], axis=0
    )
    product = jnp.dot(normed, w_ref[...], preferred_element_type=jnp.float32)
    query = head_norm(product[:, :inner], qg_ref[...], ones_ref[...])
    keys = head_norm(product[:, inner : 2 * inner], kg_ref[...], ones_ref[...])
    shape = q_ref.shape
    q_ref[...] = query.reshape(shape)
    kv_ref[0] = keys.reshape(shape)
    kv_ref[1] = product[:, 2 * inner :].astype(jnp.bfloat16).reshape(shape)


def time_attention_kernel(parts, *refs):
    queries, held, outs = refs[:parts], refs[parts : 3 * parts], refs[3 * parts + 1 :]
    cells = queries[0].shape[1]
    inner = queries[0].shape[2]
    rows = len(outs) * CELLS
    row = lax.broadcasted_iota(jnp.int32, (rows, 2 * rows), 0)
    col = lax.broadcasted_iota(jnp.int32, (rows, 2 * rows), 1)
    keep = lax.rem(row, CELLS) == lax.rem(col, CELLS)
    for b in range(cells // CELLS):
        at = slice(b * CELLS, (b + 1) * CELLS)
        query = jnp.concatenate([ref[:, at, :] for ref in queries], axis=0)

        def load(which):
            def columns(lo, hi):
                blocks = [ref[which, :, at, lo:hi] for ref in held]
                return jnp.concatenate(blocks, axis=0).reshape(2 * rows, hi - lo)

            return columns

        result = attend(query.reshape(rows, inner), load(0), load(1), inner, keep)
        result = result.astype(jnp.bfloat16).reshape(len(outs), CELLS, inner)
        for i, out in enumerate(outs):
            out[at, :] = result[i]


def gather_kernel(count, *refs):
    pieces, out_ref = refs[:count], refs[-1]
    cells = pieces[0].shape[0]
    chip = lax.axis_index("frame") // 2
    for j, ref in enumerate(pieces):
        at = lax.rem(chip, count) ^ j
        out_ref[pl.ds(pl.multiple_of(at * cells, cells), cells), :] = ref[...]


def clip_of(group, count):
    return (lax.axis_index("frame") // 2 // count) ^ group


def space_rows(blocks, clips, where, with_query, weights):
    wo_ref, norm_ref, w_ref, qg_ref, kg_ref, ones_ref = weights
    patches, inner = blocks[0].shape
    at = pl.ds(pl.multiple_of(where * patches, patches), patches)
    normed = []
    for block, clip_ref in zip(blocks, clips):
        delta = jnp.dot(block[...], wo_ref[...], preferred_element_type=jnp.float32)
        own = clip_ref[at, :].astype(jnp.float32)
        mixed = (own + delta).astype(jnp.bfloat16).astype(jnp.float32)
        normed.append(layer_norm(mixed, norm_ref[...]))
    query = None
    if with_query:
        product = jnp.dot(normed[0], w_ref[:, :inner], preferred_element_type=jnp.float32)
        query = head_norm(product, qg_ref[...], ones_ref[...])
    normed = jnp.concatenate(normed, axis=0)
    product = jnp.dot(normed, w_ref[:, inner:], preferred_element_type=jnp.float32)
    keys = head_norm(product[:, :inner], kg_ref[...], ones_ref[...])
    return query, keys, product[:, inner:].astype(jnp.bfloat16)


def space_clip_kernel(group, count, sides, *refs):
    blocks, clips, refs = refs[:sides], refs[sides : 2 * sides], refs[2 * sides :]
    weights, out_ref = refs[:6], refs[6]
    query, keys, values = space_rows(blocks, clips, clip_of(group, count), True, weights)
    inner = out_ref.shape[1]
    result = attend(
        query, lambda lo, hi: keys[:, lo:hi], lambda lo, hi: values[:, lo:hi], inner, None
    )
    out_ref[...] = result.astype(jnp.bfloat16)


def space_own_kernel(group, count, block_ref, clip_ref, *refs):
    weights, (q_ref, k_ref, v_ref) = refs[:6], refs[6:]
    q_ref[...], k_ref[...], v_ref[...] = space_rows(
        [block_ref], [clip_ref], clip_of(group, count), True, weights
    )


def space_last_kernel(group, count, others, *refs):
    blocks, clips, refs = refs[:others], refs[others : 2 * others], refs[2 * others :]
    weights, own, done, out_ref = refs[:6], refs[6:9], refs[9:-1], refs[-1]
    inner = out_ref.shape[2]
    for g, ref in enumerate(done):
        out_ref[clip_of(g, count)] = ref[...]
    where = clip_of(group, count)
    _, keys, values = space_rows(blocks, clips, where, False, weights)
    q_ref, k_ref, v_ref = own
    result = attend(
        q_ref[...],
        lambda lo, hi: jnp.concatenate([k_ref[:, lo:hi], keys[:, lo:hi]], axis=0),
        lambda lo, hi: jnp.concatenate([v_ref[:, lo:hi], values[:, lo:hi]], axis=0),
        inner,
        None,
    )
    out_ref[where] = result.astype(jnp.bfloat16)


def from_sides(array, size):
    return [
        lax.ppermute(array, "patch", [(i, (i - hop) % size) for i in range(size)])
        for hop in range(1, size)
    ]


def call(kernel, name, outs, operands, any_last=0, scratch=(), mebibytes=20, flops=0):
    bf16 = jnp.bfloat16
    shapes = [jax.ShapeDtypeStruct(shape, bf16) for shape in outs]
    results = pl.pallas_call(
        kernel,
        out_shape=shapes,
        in_specs=[VMEM] * (len(operands) - any_last) + [ANY] * any_last,
        out_specs=[VMEM] * len(outs),
        scratch_shapes=[pltpu.VMEM(shape, bf16) for shape in scratch],
        compiler_params=pltpu.CompilerParams(vmem_limit_bytes=mebibytes * MIB),
        cost_estimate=pl.CostEstimate(flops=flops, bytes_accessed=MIB, transcendentals=0),
        name=name,
    )(*operands)
    return list(results)


def body(
    sizes,
    clip,
    norm_time,
    w_time_qkv,
    q_gain_time,
    k_gain_time,
    w_time_out,
    norm_space,
    w_space_qkv,
    q_gain_space,
    k_gain_space,
):
    frames, sides = sizes
    clips, _, patches, features = clip.shape
    inner = w_time_out.shape[0]
    tokens = clips * patches
    chips = frames // 2
    cells = tokens // chips
    half = chips // 2
    count = chips // clips
    bf16 = jnp.bfloat16
    head = jnp.arange(inner) // HDIM
    ones = (head[:, None] == head[None, :]).astype(bf16)
    near, far = list(range(half)), list(range(half, chips))
    project = 2 * (tokens // 2) * features * 3 * inner * 2

    def exchange(pieces):
        moved = {0: pieces[0]}
        for k in range(1, chips):
            moved[k] = lax.ppermute(pieces[k], "frame", [(i, i ^ (2 * k)) for i in range(frames)])
        return moved

    def other_core(array):
        return lax.ppermute(array, "frame", [(i, i ^ 1) for i in range(frames)])

    rows = clip.reshape(tokens, features)
    clip_sides = [rows] + from_sides(rows, sides)
    pieces = call(
        functools.partial(pack_kernel, cells), "pack", [(cells, features)] * chips, [rows]
    )
    moved = exchange(pieces)

    time_weights = [
        norm_time.reshape(1, -1),
        w_time_qkv,
        q_gain_time.reshape(1, -1),
        k_gain_time.reshape(1, -1),
        ones,
    ]
    queries, held = [], []
    for members, name in ((near, "time_near"), (far, "time_far")):
        query, key_value = call(
            functools.partial(time_kernel, len(members)),
            name,
            [(len(members), cells, inner), (2, len(members), cells, inner)],
            [moved[k] for k in members] + time_weights + queries,
            any_last=len(queries),
            flops=project,
        )
        queries.append(query)
        held += [key_value, other_core(key_value)]
    attended = call(
        functools.partial(time_attention_kernel, 2),
        "time_attention",
        [(cells, inner)] * chips,
        queries + held + [clip_sides[-1]],
        any_last=1,
        flops=project,
    )

    back = exchange(attended)
    space_weights = [
        w_time_out,
        norm_space.reshape(1, -1),
        w_space_qkv,
        q_gain_space.reshape(1, -1),
        k_gain_space.reshape(1, -1),
        ones,
    ]
    room = 24 + 8 * (sides - 2)
    block_shape = (patches, inner)
    done = []
    for g in range(clips):
        pieces = [back[g * count + j] for j in range(count)]
        before = done[g - 2 : g - 1] if g >= 2 else []
        (block,) = call(
            functools.partial(gather_kernel, count),
            "gather",
            [block_shape],
            pieces + before,
            any_last=len(before),
        )
        others = from_sides(block, sides)
        if g < clips - 1:
            done += call(
                functools.partial(space_clip_kernel, g, count, sides),
                "space_clip",
                [block_shape],
                [block] + others + clip_sides + space_weights,
                mebibytes=room,
                flops=project,
            )
    own = call(
        functools.partial(space_own_kernel, clips - 1, count),
        "space_own",
        [block_shape] * 3,
        [block, rows] + space_weights,
        mebibytes=room,
        flops=project // 2,
    )
    (spatial,) = call(
        functools.partial(space_last_kernel, clips - 1, count, sides - 1),
        "space_last",
        [(clips, patches, inner)],
        others + clip_sides[1:] + space_weights + own + done,
        mebibytes=room,
        flops=project // 2,
    )
    return spatial.reshape(clips, 1, patches, inner)


def solution(mesh):
    sizes = (mesh.shape["frame"], mesh.shape["patch"])
    in_specs = (P(None, "frame", "patch", None),) + (P(),) * 9
    out_specs = P(None, "frame", "patch", None)
    return jax.shard_map(
        functools.partial(body, sizes),
        mesh=mesh,
        in_specs=in_specs,
        out_specs=out_specs,
        check_vma=False,
    )
```

time: 223 us -> 86 us (0.39)
  waiting for transfers between devices: 75.2 us -> 16.1 us
  local copies, waits for them, and re-layouts: 49.8 us -> 5.87 us
  matrix products: 26 us -> 0 us
  Pallas kernels: 0 us -> 25.3 us
  blocking collectives: 23 us -> 0 us
  starting transfers between devices: 17.3 us -> 37.9 us
  other arithmetic: 16.6 us -> 0.21 us
  between operations: 13.7 us -> 0.26 us
    all_gather x2 -> x0, waiting for transfers between devices: 41.1 us -> none  [the longest x1 21.4 us: body(): lax.all_gather(space_values, 'patch', axis=2, tiled=True)]
    ppermute x0 -> x21, starting transfers between devices: none -> 37.9 us  [the longest x14 30.1 us: exchange(): lax.ppermute(pieces[k], 'frame', [(i, i ^ 2 * k) for i in range(frames)])]
    all_to_all x3 -> x0, waiting for transfers between devices: 34 us -> none  [the longest x1 14.2 us: body(): lax.all_to_all(keys.reshape(local_shape), 'frame', split_axis=2, concat_a...]
    dot_general x7 -> x0, matrix products: 26 us -> none  [the longest x2 9.98 us: project_heads(): product = jnp.dot(normed, weight, preferred_element_type=jnp.float32)]
    pallas_call x0 -> x13, Pallas kernels: none -> 25.3 us  [call(): pl.pallas_call(kernel, out_shape=shapes, in_specs=[VMEM] * (len(operands)...]
    all_to_all x1 -> x0, blocking collectives: 23 us -> none  [frame_attention(): lax.all_to_all(result, 'frame', split_axis=1, concat_axis=2, tiled=True)]
    mul x12 -> x0, local copies, waits for them, and re-layouts: 18.8 us -> none  [the longest x8 11.4 us: head_norm(): scaled = split_heads * lax.rsqrt(squares + epsilon)]
    all_to_all x3 -> x0, starting transfers between devices: 17 us -> none  [the longest x1 7.4 us: body(): lax.all_to_all(keys.reshape(local_shape), 'frame', split_axis=2, concat_a...]
  transfers between devices with their start and end apart: 5 -> 21, of which waited for: 5 -> 6; matrix products, arithmetic and copies ran while one was open for 11% -> 3% of each run, Pallas kernels for 0% -> 21%
where the time goes in v1:
time: 86 us; the launch traced here: 85.8 us
  starting transfers between devices  37.9 us (44%)
  Pallas kernels  25.3 us (29%)
  waiting for transfers between devices  16.1 us (19%)
  local copies, waits for them, and re-layouts  5.87 us (7%)
    ppermute x14, starting transfers between devices, exchange(): lax.ppermute(pieces[k], 'frame', [(i, i ^ 2 * k) for i in range(frames)])  30.1 us
    pallas_call x13, Pallas kernels, call(): pl.pallas_call(kernel, out_shape=shapes, in_specs=[VMEM] * (len(operands)...  25.3 us
    ppermute x14, waiting for transfers between devices, exchange(): lax.ppermute(pieces[k], 'frame', [(i, i ^ 2 * k) for i in range(frames)])  13.6 us
    ppermute x5, starting transfers between devices, from_sides(): lax.ppermute(array, 'patch', [(i, (i - hop) % size) for i in range(size)])  7.3 us
    unnamed x18, local copies, waits for them, and re-layouts  3.78 us
    ppermute x2, waiting for transfers between devices, other_core(): return lax.ppermute(array, 'frame', [(i, i ^ 1) for i in range(frames)])  2.52 us
  transfers between devices with their start and end apart: 21, of which 6 were waited for; matrix products, arithmetic and copies ran while one was open for 3% of the time, Pallas kernels for 21%

profile of v1, /device:TPU:0, one launch (start us, length us, event | category | flops | bytes accessed | tf_op | source)
XLA Modules:
  0.0 85.8 jit_solution(17848516968794300626)
XLA Ops:
  0.0 3.0 %collective-permute-start.9 = (bf16[512,1280]{1,0:T(8,128)(2,1)}, bf16[512,1280]{1,0:T(8,128)(2,1)S(1)}, u32[]{:S(2)}, u32[]{:S(2)}) collective-permute-start(bf16[512,1280]{1,0:T(8,128)(2,1)} %bitcast.6), channel_id=1, source_target_pairs={{0,1},{1,0},{2,3},{3,2},{4,5},{5,4},{6,7},{7,6},{8,9},{9,8},{10,11... | collective-permute-start | bytes 3932168 | tf_op jit(solution)/shard_map/ppermute | solution.py:191
  3.0 1.3 %copy-done.1 = bf16[4,1,128,1280]{3,2,1,0:T(8,128)(2,1)S(1)} copy-done((bf16[4,1,128,1280]{3,2,1,0:T(8,128)(2,1)S(1)}, bf16[4,1,128,1280]{3,2,1,0:T(8,128)(2,1)}, u32[]{:S(2)}) %copy-start.1) | copy-done | bytes 1310744
  4.3 0.1 pack.1
  4.4 1.6 %collective-permute-start = (bf16[64,1280]{1,0:T(8,128)(2,1)S(1)}, bf16[64,1280]{1,0:T(8,128)(2,1)S(1)}, u32[]{:S(2)}, u32[]{:S(2)}) collective-permute-start(bf16[64,1280]{1,0:T(8,128)(2,1)S(1)} %get-tuple-element.29), channel_id=1, source_target_pairs={{0,4},{2,6},{4,0},{6,2},{8,12},{10,14},{12,8},{14,10},{16,20},{18,... | collective-permute-start | bytes 491528 | tf_op jit(solution)/shard_map/ppermute | solution.py:242
  6.0 1.6 %collective-permute-start.1 = (bf16[64,1280]{1,0:T(8,128)(2,1)S(1)}, bf16[64,1280]{1,0:T(8,128)(2,1)S(1)}, u32[]{:S(2)}, u32[]{:S(2)}) collective-permute-start(bf16[64,1280]{1,0:T(8,128)(2,1)S(1)} %get-tuple-element.30), channel_id=1, source_target_pairs={{0,8},{2,10},{4,12},{6,14},{8,0},{10,2},{12,4},{14,6},{16,24},{18,... | collective-permute-start | bytes 491528 | tf_op jit(solution)/shard_map/ppermute | solution.py:242
  7.5 0.4 collective-permute-start.2
  8.0 2.6 %collective-permute-start.3 = (bf16[64,1280]{1,0:T(8,128)(2,1)S(1)}, bf16[64,1280]{1,0:T(8,128)(2,1)S(1)}, u32[]{:S(2)}, u32[]{:S(2)}) collective-permute-start(bf16[64,1280]{1,0:T(8,128)(2,1)S(1)} %get-tuple-element.33), channel_id=1, source_target_pairs={{0,16},{2,18},{4,20},{6,22},{8,24},{10,26},{12,28},{14,30},{16,0},... | collective-permute-start | bytes 491528 | tf_op jit(solution)/shard_map/ppermute | solution.py:242
  10.6 0.7 reshape.51.refs_4_
  11.3 0.7 reshape.52.refs_6_
  12.0 0.7 reshape.53.refs_7_
  12.6 0.2 compare_convert_fusion.refs_8_.refs_9_.refs_5_.refs_7_
  12.9 1.4 %collective-permute-start.4 = (bf16[64,1280]{1,0:T(8,128)(2,1)S(1)}, bf16[64,1280]{1,0:T(8,128)(2,1)S(1)}, u32[]{:S(2)}, u32[]{:S(2)}) collective-permute-start(bf16[64,1280]{1,0:T(8,128)(2,1)S(1)} %get-tuple-element.34), channel_id=1, source_target_pairs={{0,20},{2,22},{4,16},{6,18},{8,28},{10,30},{12,24},{14,26},{16,4},... | collective-permute-start | bytes 491528 | tf_op jit(solution)/shard_map/ppermute | solution.py:242
  14.2 3.2 %collective-permute-done.1.refs_2_ = bf16[64,1280]{1,0:T(8,128)(2,1)S(1)} collective-permute-done((bf16[64,1280]{1,0:T(8,128)(2,1)S(1)}, bf16[64,1280]{1,0:T(8,128)(2,1)S(1)}, u32[]{:S(2)}, u32[]{:S(2)}) %collective-permute-start.1) | collective-permute-done | bytes 163872 | tf_op jit(solution)/shard_map/ppermute | solution.py:242
  17.4 3.3 %collective-permute-start.5 = (bf16[64,1280]{1,0:T(8,128)(2,1)S(1)}, bf16[64,1280]{1,0:T(8,128)(2,1)S(1)}, u32[]{:S(2)}, u32[]{:S(2)}) collective-permute-start(bf16[64,1280]{1,0:T(8,128)(2,1)S(1)} %get-tuple-element.35), channel_id=1, source_target_pairs={{0,24},{2,26},{4,28},{6,30},{8,16},{10,18},{12,20},{14,22},{16,8},... | collective-permute-start | bytes 491528 | tf_op jit(solution)/shard_map/ppermute | solution.py:242
  20.8 0.0 collective-permute-done.2.refs_3_
  20.8 2.7 %collective-permute-start.6 = (bf16[64,1280]{1,0:T(8,128)(2,1)S(1)}, bf16[64,1280]{1,0:T(8,128)(2,1)S(1)}, u32[]{:S(2)}, u32[]{:S(2)}) collective-permute-start(bf16[64,1280]{1,0:T(8,128)(2,1)S(1)} %get-tuple-element.36), channel_id=1, source_target_pairs={{0,28},{2,30},{4,24},{6,26},{8,20},{10,22},{12,16},{14,18},{16,12}... | collective-permute-start | bytes 491528 | tf_op jit(solution)/shard_map/ppermute | solution.py:242
  23.4 2.4 %copy-done.3 = bf16[1280,1920]{1,0:T(8,128)(2,1)S(1)} copy-done((bf16[1280,1920]{1,0:T(8,128)(2,1)S(1)}, bf16[1280,1920]{1,0:T(8,128)(2,1)}, u32[]{:S(2)}) %copy-start.3) | copy-done | bytes 4915224
  25.8 2.5 %time_near.1 = (bf16[4,64,640]{2,1,0:T(8,128)(2,1)S(1)}, bf16[2,4,64,640]{3,2,1,0:T(8,128)(2,1)S(1)}) custom-call(bf16[64,1280]{1,0:T(8,128)(2,1)S(1)} %get-tuple-element.28.refs_0_, bf16[64,1280]{1,0:T(8,128)(2,1)S(1)} %collective-permute-done.refs_1_, bf16[64,1280]{1,0:T(8,128)(2,1)S(1)} %collective-permute-done.1.refs_2_, ...), custom_call_target="tpu_custom_call" | custom-call | flops 2516582400 | bytes 1048576 | tf_op jit(solution)/shard_map/time_near/pallas_call | solution.py:199
  28.3 6.3 %collective-permute-done.4.refs_1_ = bf16[64,1280]{1,0:T(8,128)(2,1)S(1)} collective-permute-done((bf16[64,1280]{1,0:T(8,128)(2,1)S(1)}, bf16[64,1280]{1,0:T(8,128)(2,1)S(1)}, u32[]{:S(2)}, u32[]{:S(2)}) %collective-permute-start.4) | collective-permute-done | bytes 163872 | tf_op jit(solution)/shard_map/ppermute | solution.py:242
  34.5 0.0 collective-permute-done.5.refs_2_
  34.6 0.0 collective-permute-done.6.refs_3_
  34.6 2.5 %time_far.1 = (bf16[4,64,640]{2,1,0:T(8,128)(2,1)S(1)}, bf16[2,4,64,640]{3,2,1,0:T(8,128)(2,1)S(1)}) custom-call(bf16[64,1280]{1,0:T(8,128)(2,1)S(1)} %collective-permute-done.3.refs_0_, bf16[64,1280]{1,0:T(8,128)(2,1)S(1)} %collective-permute-done.4.refs_1_, bf16[64,1280]{1,0:T(8,128)(2,1)S(1)} %collective-permute-done.5.refs_2_, ...), custom_call_target="tpu_custom_call" | custom-call | flops 2516582400 | bytes 1048576 | tf_op jit(solution)/shard_map/time_far/pallas_call | solution.py:199
  37.0 0.1 collective-permute-start.8
  37.1 0.5 collective-permute-start.7
  37.6 1.6 %collective-permute-done.8.refs_5_ = bf16[2,4,64,640]{3,2,1,0:T(8,128)(2,1)S(1)} collective-permute-done((bf16[2,4,64,640]{3,2,1,0:T(8,128)(2,1)S(1)}, bf16[2,4,64,640]{3,2,1,0:T(8,128)(2,1)S(1)}, u32[]{:S(2)}, u32[]{:S(2)}) %collective-permute-start.8) | collective-permute-done | bytes 655392 | tf_op jit(solution)/shard_map/ppermute | solution.py:246
  39.2 0.9 %collective-permute-done.7.refs_3_ = bf16[2,4,64,640]{3,2,1,0:T(8,128)(2,1)S(1)} collective-permute-done((bf16[2,4,64,640]{3,2,1,0:T(8,128)(2,1)S(1)}, bf16[2,4,64,640]{3,2,1,0:T(8,128)(2,1)S(1)}, u32[]{:S(2)}, u32[]{:S(2)}) %collective-permute-start.7) | collective-permute-done | bytes 655392 | tf_op jit(solution)/shard_map/ppermute | solution.py:246
  40.2 0.0 copy-start.6
  40.2 0.0 copy-start
  40.2 0.0 copy-start.2
  40.2 4.1 %time_attention.1 = (bf16[64,640]{1,0:T(8,128)(2,1)S(1)}, bf16[64,640]{1,0:T(8,128)(2,1)S(1)}, bf16[64,640]{1,0:T(8,128)(2,1)S(1)}, bf16[64,640]{1,0:T(8,128)(2,...) custom-call(bf16[4,64,640]{2,1,0:T(8,128)(2,1)S(1)} %get-tuple-eleme, ...), custom_call_target="tpu_custom_call" | custom-call | flops 2516582400 | bytes 1048576 | tf_op jit(solution)/shard_map/time_attention/pallas_call | solution.py:199
  44.3 1.3 %collective-permute-start.16 = (bf16[64,640]{1,0:T(8,128)(2,1)S(1)}, bf16[64,640]{1,0:T(8,128)(2,1)S(1)}, u32[]{:S(2)}, u32[]{:S(2)}) collective-permute-start(bf16[64,640]{1,0:T(8,128)(2,1)S(1)} %get-tuple-element.48), channel_id=1, source_target_pairs={{0,4},{2,6},{4,0},{6,2},{8,12},{10,14},{12,8},{14,10},{16,20},{18,... | collective-permute-start | bytes 245768 | tf_op jit(solution)/shard_map/ppermute | solution.py:242
  45.6 3.3 %collective-permute-done.16.refs_1_ = bf16[64,640]{1,0:T(8,128)(2,1)S(1)} collective-permute-done((bf16[64,640]{1,0:T(8,128)(2,1)S(1)}, bf16[64,640]{1,0:T(8,128)(2,1)S(1)}, u32[]{:S(2)}, u32[]{:S(2)}) %collective-permute-start.16) | collective-permute-done | bytes 81952 | tf_op jit(solution)/shard_map/ppermute | solution.py:242
  48.9 0.6 collective-permute-start.17
  49.5 6.2 %collective-permute-start.12 = (bf16[64,640]{1,0:T(8,128)(2,1)S(1)}, bf16[64,640]{1,0:T(8,128)(2,1)S(1)}, u32[]{:S(2)}, u32[]{:S(2)}) collective-permute-start(bf16[64,640]{1,0:T(8,128)(2,1)S(1)} %get-tuple-element.42), channel_id=1, source_target_pairs={{0,8},{2,10},{4,12},{6,14},{8,0},{10,2},{12,4},{14,6},{16,24},{18,... | collective-permute-start | bytes 245768 | tf_op jit(solution)/shard_map/ppermute | solution.py:242
  55.7 0.7 collective-permute-start.13
  56.5 3.0 %collective-permute-start.18 = (bf16[64,640]{1,0:T(8,128)(2,1)S(1)}, bf16[64,640]{1,0:T(8,128)(2,1)S(1)}, u32[]{:S(2)}, u32[]{:S(2)}) collective-permute-start(bf16[64,640]{1,0:T(8,128)(2,1)S(1)} %get-tuple-element.49), channel_id=1, source_target_pairs={{0,16},{2,18},{4,20},{6,22},{8,24},{10,26},{12,28},{14,30},{16,0},... | collective-permute-start | bytes 245768 | tf_op jit(solution)/shard_map/ppermute | solution.py:242
  59.4 0.8 collective-permute-start.19
  60.2 2.5 %collective-permute-start.10 = (bf16[64,640]{1,0:T(8,128)(2,1)S(1)}, bf16[64,640]{1,0:T(8,128)(2,1)S(1)}, u32[]{:S(2)}, u32[]{:S(2)}) collective-permute-start(bf16[64,640]{1,0:T(8,128)(2,1)S(1)} %get-tuple-element.40), channel_id=1, source_target_pairs={{0,24},{2,26},{4,28},{6,30},{8,16},{10,18},{12,20},{14,22},{16,8},... | collective-permute-start | bytes 245768 | tf_op jit(solution)/shard_map/ppermute | solution.py:242
  62.7 2.2 %collective-permute-start.11 = (bf16[64,640]{1,0:T(8,128)(2,1)S(1)}, bf16[64,640]{1,0:T(8,128)(2,1)S(1)}, u32[]{:S(2)}, u32[]{:S(2)}) collective-permute-start(bf16[64,640]{1,0:T(8,128)(2,1)S(1)} %get-tuple-element.41), channel_id=1, source_target_pairs={{0,28},{2,30},{4,24},{6,26},{8,20},{10,22},{12,16},{14,18},{16,12}... | collective-permute-start | bytes 245768 | tf_op jit(solution)/shard_map/ppermute | solution.py:242
  64.9 1.6 %collective-permute-start.14 = (bf16[128,640]{1,0:T(8,128)(2,1)S(1)}, bf16[128,640]{1,0:T(8,128)(2,1)S(1)}, u32[]{:S(2)}, u32[]{:S(2)}) collective-permute-start(bf16[128,640]{1,0:T(8,128)(2,1)S(1)} %gather.4.refs_0_), channel_id=1, source_target_pairs={{0,1},{1,0},{2,3},{3,2},{4,5},{5,4},{6,7},{7,6},{8,9},{9,8},{10,11... | collective-permute-start | bytes 491528 | tf_op jit(solution)/shard_map/ppermute | solution.py:191
  66.5 3.7 %space_clip.4.refs_2_.refs_11_ = bf16[128,640]{1,0:T(8,128)(2,1)S(1)} custom-call(bf16[128,640]{1,0:T(8,128)(2,1)S(1)} %gather.6.refs_0_, bf16[128,640]{1,0:T(8,128)(2,1)S(1)} %collective-permute-done.17.refs_1_, bf16[512,1280]{1,0:T(8,128)(2,1)S(1)} %bitcast.8, bf16[512,1280]{1,0:T(8,128)(2,1)S(1)} %collective-permute-done.9.refs_6_.refs_3_.refs_1_, ...), custom_call_target="tpu_custom_call" | custom-call | flops 2516582400 | bytes 1048576 | tf_op jit(solution)/shard_map/space_clip/pallas_call | solution.py:199
  70.2 0.9 %collective-permute-done.19.refs_1_ = bf16[64,640]{1,0:T(8,128)(2,1)S(1)} collective-permute-done((bf16[64,640]{1,0:T(8,128)(2,1)S(1)}, bf16[64,640]{1,0:T(8,128)(2,1)S(1)}, u32[]{:S(2)}, u32[]{:S(2)}) %collective-permute-start.19) | collective-permute-done | bytes 81952 | tf_op jit(solution)/shard_map/ppermute | solution.py:242
  71.1 1.7 %collective-permute-start.20 = (bf16[128,640]{1,0:T(8,128)(2,1)S(1)}, bf16[128,640]{1,0:T(8,128)(2,1)S(1)}, u32[]{:S(2)}, u32[]{:S(2)}) collective-permute-start(bf16[128,640]{1,0:T(8,128)(2,1)S(1)} %gather.7.refs_0_), channel_id=1, source_target_pairs={{0,1},{1,0},{2,3},{3,2},{4,5},{5,4},{6,7},{7,6},{8,9},{9,8},{10,11... | collective-permute-start | bytes 491528 | tf_op jit(solution)/shard_map/ppermute | solution.py:191
  72.8 3.5 %space_clip.3.refs_2_.refs_12_ = bf16[128,640]{1,0:T(8,128)(2,1)S(1)} custom-call(bf16[128,640]{1,0:T(8,128)(2,1)S(1)} %gather.4.refs_0_, bf16[128,640]{1,0:T(8,128)(2,1)S(1)} %collective-permute-done.14.refs_1_, bf16[512,1280]{1,0:T(8,128)(2,1)S(1)} %bitcast.9, bf16[512,1280]{1,0:T(8,128)(2,1)S(1)} %collective-permute-done.9.refs_6_.refs_3_.refs_1_, ...), custom_call_target="tpu_custom_call" | custom-call | flops 2516582400 | bytes 1048576 | tf_op jit(solution)/shard_map/space_clip/pallas_call | solution.py:199
  76.4 0.5 collective-permute-start.15
  76.9 1.9 %space_own.1 = (bf16[128,640]{1,0:T(8,128)(2,1)S(1)}, bf16[128,640]{1,0:T(8,128)(2,1)S(1)}, bf16[128,640]{1,0:T(8,128)(2,1)S(1)}) custom-call(bf16[128,640]{1,0:T(8,128)(2,1)S(1)} %gather.5.block_ref, bf16[512,1280]{1,0:T(8,128)(2,1)S(1)} %bitcast.10, bf16[640,1280]{1,0:T(8,128)(2,1)S(1)} %copy-done, f32[1,1280]{1,0:T(1,128)S(1)} %reshape.54.refs_5_.refs_1_.refs_3_, ...), custom_call_target="tpu_custom_call" | custom-call | flops 1258291200 | bytes 1048576 | tf_op jit(solution)/shard_map/space_own/pallas_call | solution.py:199
  78.8 3.5 %space_clip.5.refs_13_ = bf16[128,640]{1,0:T(8,128)(2,1)S(1)} custom-call(bf16[128,640]{1,0:T(8,128)(2,1)S(1)} %gather.7.refs_0_, bf16[128,640]{1,0:T(8,128)(2,1)S(1)} %collective-permute-done.20.refs_1_, bf16[512,1280]{1,0:T(8,128)(2,1)S(1)} %bitcast.11, bf16[512,1280]{1,0:T(8,128)(2,1)S(1)} %collective-permute-done.9.refs_6_.refs_3_.refs_1_, ...), custom_call_target="tpu_custom_call" | custom-call | flops 2516582400 | bytes 1048576 | tf_op jit(solution)/shard_map/space_clip/pallas_call | solution.py:199
  82.4 3.4 %space_last.1 = bf16[4,128,640]{2,1,0:T(8,128)(2,1)} custom-call(bf16[128,640]{1,0:T(8,128)(2,1)S(1)} %collective-permute-done.15.refs_0_, bf16[512,1280]{1,0:T(8,128)(2,1)S(1)} %collective-permute-done.9.refs_6_.refs_3_.refs_1_, bf16[640,1280]{1,0:T(8,128)(2,1)S(1)} %copy-done, f32[1,1280]{1,0:T(1,128)S(1)} %reshape.54.refs_5_.refs_1_.refs_3_, ...), custom_call_target="tpu_custom_call" | custom-call | flops 1258291200 | bytes 1048576 | tf_op jit(solution)/shard_map/space_last/pallas_call | solution.py:199
  (34 shorter events, 0.2 us)
Async XLA Ops:
  0.0 40.1 %collective-permute-start.9 = (bf16[512,1280]{1,0:T(8,128)(2,1)}, bf16[512,1280]{1,0:T(8,128)(2,1)S(1)}, u32[]{:S(2)}, u32[]{:S(2)}) collective-permute-start(bf16[512,1280]{1,0:T(8,128)(2,1)} %bitcast.6), channel_id=1, source_target_pairs={{0,1},{1,0},{2,3},{3,2},{4,5},{5,4},{6,7},{7,6},{8,9},{9,8},{10,11... | collective-permute-start | bytes 3932168 | tf_op jit(solution)/shard_map/ppermute | solution.py:191
  3.0 1.4 %copy-start.1 = (bf16[4,1,128,1280]{3,2,1,0:T(8,128)(2,1)S(1)}, bf16[4,1,128,1280]{3,2,1,0:T(8,128)(2,1)}, u32[]{:S(2)}) copy-start(bf16[4,1,128,1280]{3,2,1,0:T(8,128)(2,1)} %param.10) | copy-start | bytes 3932164
  4.4 8.4 %collective-permute-start = (bf16[64,1280]{1,0:T(8,128)(2,1)S(1)}, bf16[64,1280]{1,0:T(8,128)(2,1)S(1)}, u32[]{:S(2)}, u32[]{:S(2)}) collective-permute-start(bf16[64,1280]{1,0:T(8,128)(2,1)S(1)} %get-tuple-element.29), channel_id=1, source_target_pairs={{0,4},{2,6},{4,0},{6,2},{8,12},{10,14},{12,8},{14,10},{16,20},{18,... | collective-permute-start | bytes 491528 | tf_op jit(solution)/shard_map/ppermute | solution.py:242
  6.0 11.5 %collective-permute-start.1 = (bf16[64,1280]{1,0:T(8,128)(2,1)S(1)}, bf16[64,1280]{1,0:T(8,128)(2,1)S(1)}, u32[]{:S(2)}, u32[]{:S(2)}) collective-permute-start(bf16[64,1280]{1,0:T(8,128)(2,1)S(1)} %get-tuple-element.30), channel_id=1, source_target_pairs={{0,8},{2,10},{4,12},{6,14},{8,0},{10,2},{12,4},{14,6},{16,24},{18,... | collective-permute-start | bytes 491528 | tf_op jit(solution)/shard_map/ppermute | solution.py:242
  7.5 13.2 %collective-permute-start.2 = (bf16[64,1280]{1,0:T(8,128)(2,1)S(1)}, bf16[64,1280]{1,0:T(8,128)(2,1)S(1)}, u32[]{:S(2)}, u32[]{:S(2)}) collective-permute-start(bf16[64,1280]{1,0:T(8,128)(2,1)S(1)} %get-tuple-element.31), channel_id=1, source_target_pairs={{0,12},{2,14},{4,8},{6,10},{8,4},{10,6},{12,0},{14,2},{16,28},{18,... | collective-permute-start | bytes 491528 | tf_op jit(solution)/shard_map/ppermute | solution.py:242
  8.0 20.3 %collective-permute-start.3 = (bf16[64,1280]{1,0:T(8,128)(2,1)S(1)}, bf16[64,1280]{1,0:T(8,128)(2,1)S(1)}, u32[]{:S(2)}, u32[]{:S(2)}) collective-permute-start(bf16[64,1280]{1,0:T(8,128)(2,1)S(1)} %get-tuple-element.33), channel_id=1, source_target_pairs={{0,16},{2,18},{4,20},{6,22},{8,24},{10,26},{12,28},{14,30},{16,0},... | collective-permute-start | bytes 491528 | tf_op jit(solution)/shard_map/ppermute | solution.py:242
  12.9 21.7 %collective-permute-start.4 = (bf16[64,1280]{1,0:T(8,128)(2,1)S(1)}, bf16[64,1280]{1,0:T(8,128)(2,1)S(1)}, u32[]{:S(2)}, u32[]{:S(2)}) collective-permute-start(bf16[64,1280]{1,0:T(8,128)(2,1)S(1)} %get-tuple-element.34), channel_id=1, source_target_pairs={{0,20},{2,22},{4,16},{6,18},{8,28},{10,30},{12,24},{14,26},{16,4},... | collective-permute-start | bytes 491528 | tf_op jit(solution)/shard_map/ppermute | solution.py:242
  17.4 17.1 %collective-permute-start.5 = (bf16[64,1280]{1,0:T(8,128)(2,1)S(1)}, bf16[64,1280]{1,0:T(8,128)(2,1)S(1)}, u32[]{:S(2)}, u32[]{:S(2)}) collective-permute-start(bf16[64,1280]{1,0:T(8,128)(2,1)S(1)} %get-tuple-element.35), channel_id=1, source_target_pairs={{0,24},{2,26},{4,28},{6,30},{8,16},{10,18},{12,20},{14,22},{16,8},... | collective-permute-start | bytes 491528 | tf_op jit(solution)/shard_map/ppermute | solution.py:242
  20.8 13.8 %collective-permute-start.6 = (bf16[64,1280]{1,0:T(8,128)(2,1)S(1)}, bf16[64,1280]{1,0:T(8,128)(2,1)S(1)}, u32[]{:S(2)}, u32[]{:S(2)}) collective-permute-start(bf16[64,1280]{1,0:T(8,128)(2,1)S(1)} %get-tuple-element.36), channel_id=1, source_target_pairs={{0,28},{2,30},{4,24},{6,26},{8,20},{10,22},{12,16},{14,18},{16,12}... | collective-permute-start | bytes 491528 | tf_op jit(solution)/shard_map/ppermute | solution.py:242
  23.4 2.4 %copy-start.3 = (bf16[1280,1920]{1,0:T(8,128)(2,1)S(1)}, bf16[1280,1920]{1,0:T(8,128)(2,1)}, u32[]{:S(2)}) copy-start(bf16[1280,1920]{1,0:T(8,128)(2,1)} %refs_5_.3) | copy-start | bytes 14745604
  37.0 2.2 %collective-permute-start.8 = (bf16[2,4,64,640]{3,2,1,0:T(8,128)(2,1)S(1)}, bf16[2,4,64,640]{3,2,1,0:T(8,128)(2,1)S(1)}, u32[]{:S(2)}, u32[]{:S(2)}) collective-permute-start(bf16[2,4,64,640]{3,2,1,0:T(8,128)(2,1)S(1)} %get-tuple-element.39.refs_4_), channel_id=1, source_target_pairs={{0,2},{2,0},{4,6},{6,4},{8,10},{10,8},{12,14},{14,12},{16,18},{18,... | collective-permute-start | bytes 1966088 | tf_op jit(solution)/shard_map/ppermute | solution.py:246
  37.1 3.0 %collective-permute-start.7 = (bf16[2,4,64,640]{3,2,1,0:T(8,128)(2,1)S(1)}, bf16[2,4,64,640]{3,2,1,0:T(8,128)(2,1)S(1)}, u32[]{:S(2)}, u32[]{:S(2)}) collective-permute-start(bf16[2,4,64,640]{3,2,1,0:T(8,128)(2,1)S(1)} %get-tuple-element.38.refs_2_), channel_id=1, source_target_pairs={{0,2},{2,0},{4,6},{6,4},{8,10},{10,8},{12,14},{14,12},{16,18},{18,... | collective-permute-start | bytes 1966088 | tf_op jit(solution)/shard_map/ppermute | solution.py:246
  40.2 26.3 %slice-start = ((s8[4915200]{0:T(1024)(128)(4,1)}), s8[4194304]{0:T(1024)(128)(4,1)S(1)}, s32[]{:S(2)}) async-start(s8[4915200]{0:T(1024)(128)(4,1)} %bitcast.4), calls=%async_computation | async-start | bytes 8388608
  40.2 16.3 %copy-start.4 = (f32[1280]{0:T(1024)S(1)}, f32[1280]{0:T(1024)}, u32[]{:S(2)}) copy-start(f32[1280]{0:T(1024)} %param.16) | copy-start | bytes 15364
  40.2 16.3 %copy-start.5 = (f32[640]{0:T(1024)S(1)}, f32[640]{0:T(1024)}, u32[]{:S(2)}) copy-start(f32[640]{0:T(1024)} %param.18) | copy-start | bytes 7684
  40.2 16.3 %copy-start.6 = (f32[640]{0:T(1024)S(1)}, f32[640]{0:T(1024)}, u32[]{:S(2)}) copy-start(f32[640]{0:T(1024)} %param.19) | copy-start | bytes 7684
  40.2 26.3 %slice-start.1 = ((s8[4915200]{0:T(1024)(128)(4,1)}), s8[720896]{0:T(1024)(128)(4,1)S(1)}, s32[]{:S(2)}) async-start(s8[4915200]{0:T(1024)(128)(4,1)} %bitcast.4), calls=%async_computation.1 | async-start | bytes 1441792
  40.2 26.3 %copy-start = (bf16[640,1280]{1,0:T(8,128)(2,1)S(1)}, bf16[640,1280]{1,0:T(8,128)(2,1)}, u32[]{:S(2)}) copy-start(bf16[640,1280]{1,0:T(8,128)(2,1)} %refs_2_.3) | copy-start | bytes 4915204
  40.2 26.3 %copy-start.2 = (bf16[4,1,128,1280]{3,2,1,0:T(8,128)(2,1)S(1)}, bf16[4,1,128,1280]{3,2,1,0:T(8,128)(2,1)}, u32[]{:S(2)}) copy-start(bf16[4,1,128,1280]{3,2,1,0:T(8,128)(2,1)} %param.10) | copy-start | bytes 3932164
  44.3 4.5 %collective-permute-start.16 = (bf16[64,640]{1,0:T(8,128)(2,1)S(1)}, bf16[64,640]{1,0:T(8,128)(2,1)S(1)}, u32[]{:S(2)}, u32[]{:S(2)}) collective-permute-start(bf16[64,640]{1,0:T(8,128)(2,1)S(1)} %get-tuple-element.48), channel_id=1, source_target_pairs={{0,4},{2,6},{4,0},{6,2},{8,12},{10,14},{12,8},{14,10},{16,20},{18,... | collective-permute-start | bytes 245768 | tf_op jit(solution)/shard_map/ppermute | solution.py:242
  48.9 16.0 %collective-permute-start.17 = (bf16[128,640]{1,0:T(8,128)(2,1)S(1)}, bf16[128,640]{1,0:T(8,128)(2,1)S(1)}, u32[]{:S(2)}, u32[]{:S(2)}) collective-permute-start(bf16[128,640]{1,0:T(8,128)(2,1)S(1)} %gather.6.refs_0_), channel_id=1, source_target_pairs={{0,1},{1,0},{2,3},{3,2},{4,5},{5,4},{6,7},{7,6},{8,9},{9,8},{10,11... | collective-permute-start | bytes 491528 | tf_op jit(solution)/shard_map/ppermute | solution.py:191
  49.5 10.7 %collective-permute-start.12 = (bf16[64,640]{1,0:T(8,128)(2,1)S(1)}, bf16[64,640]{1,0:T(8,128)(2,1)S(1)}, u32[]{:S(2)}, u32[]{:S(2)}) collective-permute-start(bf16[64,640]{1,0:T(8,128)(2,1)S(1)} %get-tuple-element.42), channel_id=1, source_target_pairs={{0,8},{2,10},{4,12},{6,14},{8,0},{10,2},{12,4},{14,6},{16,24},{18,... | collective-permute-start | bytes 245768 | tf_op jit(solution)/shard_map/ppermute | solution.py:242
  55.7 7.0 %collective-permute-start.13 = (bf16[64,640]{1,0:T(8,128)(2,1)S(1)}, bf16[64,640]{1,0:T(8,128)(2,1)S(1)}, u32[]{:S(2)}, u32[]{:S(2)}) collective-permute-start(bf16[64,640]{1,0:T(8,128)(2,1)S(1)} %get-tuple-element.43), channel_id=1, source_target_pairs={{0,12},{2,14},{4,8},{6,10},{8,4},{10,6},{12,0},{14,2},{16,28},{18,... | collective-permute-start | bytes 245768 | tf_op jit(solution)/shard_map/ppermute | solution.py:242
  56.5 13.7 %collective-permute-start.18 = (bf16[64,640]{1,0:T(8,128)(2,1)S(1)}, bf16[64,640]{1,0:T(8,128)(2,1)S(1)}, u32[]{:S(2)}, u32[]{:S(2)}) collective-permute-start(bf16[64,640]{1,0:T(8,128)(2,1)S(1)} %get-tuple-element.49), channel_id=1, source_target_pairs={{0,16},{2,18},{4,20},{6,22},{8,24},{10,26},{12,28},{14,30},{16,0},... | collective-permute-start | bytes 245768 | tf_op jit(solution)/shard_map/ppermute | solution.py:242
  59.4 11.7 %collective-permute-start.19 = (bf16[64,640]{1,0:T(8,128)(2,1)S(1)}, bf16[64,640]{1,0:T(8,128)(2,1)S(1)}, u32[]{:S(2)}, u32[]{:S(2)}) collective-permute-start(bf16[64,640]{1,0:T(8,128)(2,1)S(1)} %get-tuple-element.50), channel_id=1, source_target_pairs={{0,20},{2,22},{4,16},{6,18},{8,28},{10,30},{12,24},{14,26},{16,4},... | collective-permute-start | bytes 245768 | tf_op jit(solution)/shard_map/ppermute | solution.py:242
  60.2 16.2 %collective-permute-start.10 = (bf16[64,640]{1,0:T(8,128)(2,1)S(1)}, bf16[64,640]{1,0:T(8,128)(2,1)S(1)}, u32[]{:S(2)}, u32[]{:S(2)}) collective-permute-start(bf16[64,640]{1,0:T(8,128)(2,1)S(1)} %get-tuple-element.40), channel_id=1, source_target_pairs={{0,24},{2,26},{4,28},{6,30},{8,16},{10,18},{12,20},{14,22},{16,8},... | collective-permute-start | bytes 245768 | tf_op jit(solution)/shard_map/ppermute | solution.py:242
  62.7 13.7 %collective-permute-start.11 = (bf16[64,640]{1,0:T(8,128)(2,1)S(1)}, bf16[64,640]{1,0:T(8,128)(2,1)S(1)}, u32[]{:S(2)}, u32[]{:S(2)}) collective-permute-start(bf16[64,640]{1,0:T(8,128)(2,1)S(1)} %get-tuple-element.41), channel_id=1, source_target_pairs={{0,28},{2,30},{4,24},{6,26},{8,20},{10,22},{12,16},{14,18},{16,12}... | collective-permute-start | bytes 245768 | tf_op jit(solution)/shard_map/ppermute | solution.py:242
  64.9 7.9 %collective-permute-start.14 = (bf16[128,640]{1,0:T(8,128)(2,1)S(1)}, bf16[128,640]{1,0:T(8,128)(2,1)S(1)}, u32[]{:S(2)}, u32[]{:S(2)}) collective-permute-start(bf16[128,640]{1,0:T(8,128)(2,1)S(1)} %gather.4.refs_0_), channel_id=1, source_target_pairs={{0,1},{1,0},{2,3},{3,2},{4,5},{5,4},{6,7},{7,6},{8,9},{9,8},{10,11... | collective-permute-start | bytes 491528 | tf_op jit(solution)/shard_map/ppermute | solution.py:191
  71.1 7.7 %collective-permute-start.20 = (bf16[128,640]{1,0:T(8,128)(2,1)S(1)}, bf16[128,640]{1,0:T(8,128)(2,1)S(1)}, u32[]{:S(2)}, u32[]{:S(2)}) collective-permute-start(bf16[128,640]{1,0:T(8,128)(2,1)S(1)} %gather.7.refs_0_), channel_id=1, source_target_pairs={{0,1},{1,0},{2,3},{3,2},{4,5},{5,4},{6,7},{7,6},{8,9},{9,8},{10,11... | collective-permute-start | bytes 491528 | tf_op jit(solution)/shard_map/ppermute | solution.py:191
  76.4 6.0 %collective-permute-start.15 = (bf16[128,640]{1,0:T(8,128)(2,1)S(1)}, bf16[128,640]{1,0:T(8,128)(2,1)S(1)}, u32[]{:S(2)}, u32[]{:S(2)}) collective-permute-start(bf16[128,640]{1,0:T(8,128)(2,1)S(1)} %gather.5.block_ref), channel_id=1, source_target_pairs={{0,1},{1,0},{2,3},{3,2},{4,5},{5,4},{6,7},{7,6},{8,9},{9,8},{10,11... | collective-permute-start | bytes 491528 | tf_op jit(solution)/shard_map/ppermute | solution.py:191

commit v2 on v1

--- a/solution.py
+++ b/solution.py
@@ -36,32 +36,38 @@
 
 def attend(query, load_keys, load_values, inner, keep):
     rows = query.shape[0]
-    tiles = [None] * (inner // LANES)
+    spans, masks, scores, exponents, totals = [], [], [], [], []
     for head in range(inner // HDIM):
         first, last = head * HDIM // LANES, ((head + 1) * HDIM - 1) // LANES
-        lo, hi = first * LANES, (last + 1) * LANES
-        masks = [lanes_of(head, tile, rows) for tile in range(first, last + 1)]
-        own = jnp.concatenate(
-            [
-                jnp.where(mask, query[:, t * LANES : (t + 1) * LANES], jnp.zeros((), query.dtype))
-                for mask, t in zip(masks, range(first, last + 1))
-            ],
-            axis=1,
+        spans.append((first, last + 1))
+        masks.append([lanes_of(head, tile, rows) for tile in range(first, last + 1)])
+        own = [
+            jnp.where(mask, query[:, t * LANES : (t + 1) * LANES], jnp.zeros((), query.dtype))
+            for mask, t in zip(masks[-1], range(first, last + 1))
+        ]
+        keys = load_keys(first * LANES, (last + 1) * LANES)
+        scores.append(
+            lax.dot_general(
+                jnp.concatenate(own, axis=1),
+                keys,
+                (((1,), (1,)), ((), ())),
+                preferred_element_type=jnp.float32,
+            )
         )
-        scores = lax.dot_general(
-            own, load_keys(lo, hi), (((1,), (1,)), ((), ())), preferred_element_type=jnp.float32
-        )
-        exponent = jnp.exp(scores * HDIM ** (-0.5))
+    for score in scores:
+        exponent = jnp.exp(score * HDIM ** (-0.5))
         if keep is not None:
             exponent = jnp.where(keep, exponent, 0.0)
-        total = jnp.sum(exponent, axis=-1, keepdims=True)
-        summed = jnp.dot(
-            exponent.astype(jnp.bfloat16), load_values(lo, hi), preferred_element_type=jnp.float32
-        )
+        totals.append(jnp.sum(exponent, axis=-1, keepdims=True))
+        exponents.append(exponent.astype(jnp.bfloat16))
+    tiles = [None] * (inner // LANES)
+    for (first, end), mask, exponent, total in zip(spans, masks, exponents, totals):
+        values = load_values(first * LANES, end * LANES)
+        summed = jnp.dot(exponent, values, preferred_element_type=jnp.float32)
         result = summed * (1.0 / total)
-        for i, t in enumerate(range(first, last + 1)):
+        for i, t in enumerate(range(first, end)):
             piece = result[:, i * LANES : (i + 1) * LANES]
-            tiles[t] = piece if tiles[t] is None else jnp.where(masks[i], piece, tiles[t])
+            tiles[t] = piece if tiles[t] is None else jnp.where(mask[i], piece, tiles[t])
     return jnp.concatenate(tiles, axis=1)
 
 
@@ -92,16 +98,15 @@
 
 
 def time_attention_kernel(parts, *refs):
-    queries, held, outs = refs[:parts], refs[parts : 3 * parts], refs[3 * parts + 1 :]
-    cells = queries[0].shape[1]
-    inner = queries[0].shape[2]
-    rows = len(outs) * CELLS
+    queries, held, outs = refs[:2], refs[2:6], refs[7:]
+    count, cells, inner = outs[0].shape
+    rows = count * len(outs) * CELLS
     row = lax.broadcasted_iota(jnp.int32, (rows, 2 * rows), 0)
     col = lax.broadcasted_iota(jnp.int32, (rows, 2 * rows), 1)
     keep = lax.rem(row, CELLS) == lax.rem(col, CELLS)
     for b in range(cells // CELLS):
         at = slice(b * CELLS, (b + 1) * CELLS)
-        query = jnp.concatenate([ref[:, at, :] for ref in queries], axis=0)
+        query = jnp.concatenate([ref[:, at, :] for ref in queries], axis=0).reshape(rows, inner)
 
         def load(which):
             def columns(lo, hi):
@@ -110,10 +115,9 @@
 
             return columns
 
-        result = attend(query.reshape(rows, inner), load(0), load(1), inner, keep)
-        result = result.astype(jnp.bfloat16).reshape(len(outs), CELLS, inner)
-        for i, out in enumerate(outs):
-            out[at, :] = result[i]
+        result = attend(query, load(0), load(1), inner, keep).astype(jnp.bfloat16)
+        for i, k in enumerate(parts[0] + parts[1]):
+            outs[k // count][k % count, at, :] = result[i * CELLS : (i + 1) * CELLS]
 
 
 def gather_kernel(count, *refs):
@@ -123,6 +127,10 @@
     for j, ref in enumerate(pieces):
         at = lax.rem(chip, count) ^ j
         out_ref[pl.ds(pl.multiple_of(at * cells, cells), cells), :] = ref[...]
+
+
+def relay_kernel(which, landed_ref, *refs):
+    refs[-1][...] = landed_ref[which]
 
 
 def clip_of(group, count):
@@ -151,7 +159,7 @@
 
 def space_clip_kernel(group, count, sides, *refs):
     blocks, clips, refs = refs[:sides], refs[sides : 2 * sides], refs[2 * sides :]
-    weights, out_ref = refs[:6], refs[6]
+    weights, out_ref = refs[:6], refs[-1]
     query, keys, values = space_rows(blocks, clips, clip_of(group, count), True, weights)
     inner = out_ref.shape[1]
     result = attend(
@@ -167,13 +175,13 @@
     )
 
 
-def space_last_kernel(group, count, others, *refs):
+def space_last_kernel(order, count, others, *refs):
     blocks, clips, refs = refs[:others], refs[others : 2 * others], refs[2 * others :]
     weights, own, done, out_ref = refs[:6], refs[6:9], refs[9:-1], refs[-1]
     inner = out_ref.shape[2]
-    for g, ref in enumerate(done):
+    for g, ref in zip(order, done):
         out_ref[clip_of(g, count)] = ref[...]
-    where = clip_of(group, count)
+    where = clip_of(order[-1], count)
     _, keys, values = space_rows(blocks, clips, where, False, weights)
     q_ref, k_ref, v_ref = own
     result = attend(
@@ -233,13 +241,20 @@
     bf16 = jnp.bfloat16
     head = jnp.arange(inner) // HDIM
     ones = (head[:, None] == head[None, :]).astype(bf16)
-    near, far = list(range(half)), list(range(half, chips))
+    quarter = max(1, half // 2)
+    parts = [
+        list(range(half, half + quarter)) + list(range(quarter)),
+        list(range(half + quarter, chips)) + list(range(quarter, half)),
+    ]
+    order = list(range(clips))
     project = 2 * (tokens // 2) * features * 3 * inner * 2
 
     def exchange(pieces):
         moved = {0: pieces[0]}
-        for k in range(1, chips):
-            moved[k] = lax.ppermute(pieces[k], "frame", [(i, i ^ (2 * k)) for i in range(frames)])
+        for k in parts[0] + parts[1]:
+            if k:
+                pairs = [(i, i ^ (2 * k)) for i in range(frames)]
+                moved[k] = lax.ppermute(pieces[k], "frame", pairs)
         return moved
 
     def other_core(array):
@@ -260,7 +275,7 @@
         ones,
     ]
     queries, held = [], []
-    for members, name in ((near, "time_near"), (far, "time_far")):
+    for members, name in zip(parts, ("time_first", "time_second")):
         query, key_value = call(
             functools.partial(time_kernel, len(members)),
             name,
@@ -272,15 +287,18 @@
         queries.append(query)
         held += [key_value, other_core(key_value)]
     attended = call(
-        functools.partial(time_attention_kernel, 2),
+        functools.partial(time_attention_kernel, parts),
         "time_attention",
-        [(cells, inner)] * chips,
+        [(count, cells, inner)] * clips,
         queries + held + [clip_sides[-1]],
         any_last=1,
         flops=project,
     )
 
-    back = exchange(attended)
+    def step_to(array, k):
+        return lax.ppermute(array, "frame", [(i, i ^ (2 * k)) for i in range(frames)])
+
+    landed = {g: step_to(attended[g], g * count) if g else attended[0] for g in order}
     space_weights = [
         w_time_out,
         norm_space.reshape(1, -1),
@@ -292,28 +310,32 @@
     room = 24 + 8 * (sides - 2)
     block_shape = (patches, inner)
     done = []
-    for g in range(clips):
-        pieces = [back[g * count + j] for j in range(count)]
-        before = done[g - 2 : g - 1] if g >= 2 else []
-        (block,) = call(
-            functools.partial(gather_kernel, count),
-            "gather",
-            [block_shape],
-            pieces + before,
-            any_last=len(before),
-        )
+    for step, g in enumerate(order):
+        pieces = [landed[g][0]]
+        before = done[1:2] if step >= 2 else []
+        for j in range(1, count):
+            relayed = call(
+                functools.partial(relay_kernel, j),
+                "relay",
+                [(cells, inner)],
+                [landed[g]] + before,
+                any_last=len(before),
+            )
+            pieces.append(step_to(relayed[0], j))
+        (block,) = call(functools.partial(gather_kernel, count), "gather", [block_shape], pieces)
         others = from_sides(block, sides)
-        if g < clips - 1:
+        if step < clips - 1:
             done += call(
                 functools.partial(space_clip_kernel, g, count, sides),
                 "space_clip",
                 [block_shape],
-                [block] + others + clip_sides + space_weights,
+                [block] + others + clip_sides + space_weights + (done[step - 1 :] if step else []),
+                any_last=len(done[step - 1 :]) if step else 0,
                 mebibytes=room,
                 flops=project,
             )
     own = call(
-        functools.partial(space_own_kernel, clips - 1, count),
+        functools.partial(space_own_kernel, order[-1], count),
         "space_own",
         [block_shape] * 3,
         [block, rows] + space_weights,
@@ -321,7 +343,7 @@
         flops=project // 2,
     )
     (spatial,) = call(
-        functools.partial(space_last_kernel, clips - 1, count, sides - 1),
+        functools.partial(space_last_kernel, order, count, sides - 1),
         "space_last",
         [(clips, patches, inner)],
         others + clip_sides[1:] + space_weights + own + done,

time: 86 us -> 84.5 us (0.983)
  waiting for transfers between devices: 16.1 us -> 27.2 us
  starting transfers between devices: 37.9 us -> 30.1 us
  Pallas kernels: 25.3 us -> 20.6 us
    ppermute x14, waiting for transfers between devices: 13.6 us -> 21.6 us  [the longest x7 12.6 us: exchange(): moved[k] = lax.ppermute(pieces[k], 'frame', pairs)]
    ppermute x14, starting transfers between devices: 30.1 us -> 24 us  [the longest x7 13.4 us: exchange(): moved[k] = lax.ppermute(pieces[k], 'frame', pairs)]
    pallas_call x13 -> x17, Pallas kernels: 25.3 us -> 20.6 us  [call(): pl.pallas_call(kernel, out_shape=shapes, in_specs=[VMEM] * (len(operands)...]
    ppermute x5, waiting for transfers between devices: 0.01 us -> 3.08 us  [from_sides(): lax.ppermute(array, 'patch', [(i, (i - hop) % size) for i in range(size)])]
    ppermute x5, starting transfers between devices: 7.3 us -> 5.53 us  [from_sides(): lax.ppermute(array, 'patch', [(i, (i - hop) % size) for i in range(size)])]
  transfers between devices with their start and end apart: 21 -> 21, of which waited for: 6 -> 11; matrix products, arithmetic and copies ran while one was open for 3% -> 3% of each run, Pallas kernels for 21% -> 19%
where the time goes in v2:
time: 84.5 us; the launch traced here: 84.2 us
  starting transfers between devices  30.1 us (36%)
  waiting for transfers between devices  27.2 us (32%)
  Pallas kernels  20.6 us (24%)
  local copies, waits for them, and re-layouts  5.89 us (7%)
    pallas_call x17, Pallas kernels, call(): pl.pallas_call(kernel, out_shape=shapes, in_specs=[VMEM] * (len(operands)...  20.6 us
    ppermute x7, starting transfers between devices, exchange(): moved[k] = lax.ppermute(pieces[k], 'frame', pairs)  13.4 us
    ppermute x7, waiting for transfers between devices, exchange(): moved[k] = lax.ppermute(pieces[k], 'frame', pairs)  12.6 us
    ppermute x7, starting transfers between devices, step_to(): return lax.ppermute(array, 'frame', [(i, i ^ 2 * k) for i in range(frames)])  10.6 us
    ppermute x7, waiting for transfers between devices, step_to(): return lax.ppermute(array, 'frame', [(i, i ^ 2 * k) for i in range(frames)])  9.06 us
    ppermute x5, starting transfers between devices, from_sides(): lax.ppermute(array, 'patch', [(i, (i - hop) % size) for i in range(size)])  5.53 us
    unnamed x18, local copies, waits for them, and re-layouts  3.77 us
    ppermute x5, waiting for transfers between devices, from_sides(): lax.ppermute(array, 'patch', [(i, (i - hop) % size) for i in range(size)])  3.08 us
  transfers between devices with their start and end apart: 21, of which 11 were waited for; matrix products, arithmetic and copies ran while one was open for 3% of the time, Pallas kernels for 19%

profile of v2, /device:TPU:0, one launch (start us, length us, event | category | flops | bytes accessed | tf_op | source)
XLA Modules:
  0.0 84.2 jit_solution(12668431250986255423)
XLA Ops:
  0.0 3.0 %collective-permute-start.9 = (bf16[512,1280]{1,0:T(8,128)(2,1)}, bf16[512,1280]{1,0:T(8,128)(2,1)S(1)}, u32[]{:S(2)}, u32[]{:S(2)}) collective-permute-start(bf16[512,1280]{1,0:T(8,128)(2,1)} %bitcast.14), channel_id=1, source_target_pairs={{0,1},{1,0},{2,3},{3,2},{4,5},{5,4},{6,7},{7,6},{8,9},{9,8},{10,11... | collective-permute-start | bytes 3932168 | tf_op jit(solution)/shard_map/ppermute | solution.py:199
  3.0 1.3 %copy-done.1 = bf16[4,1,128,1280]{3,2,1,0:T(8,128)(2,1)S(1)} copy-done((bf16[4,1,128,1280]{3,2,1,0:T(8,128)(2,1)S(1)}, bf16[4,1,128,1280]{3,2,1,0:T(8,128)(2,1)}, u32[]{:S(2)}) %copy-start.1) | copy-done | bytes 1310744
  4.3 0.1 pack.1
  4.4 2.7 %collective-permute-start = (bf16[64,1280]{1,0:T(8,128)(2,1)S(1)}, bf16[64,1280]{1,0:T(8,128)(2,1)S(1)}, u32[]{:S(2)}, u32[]{:S(2)}) collective-permute-start(bf16[64,1280]{1,0:T(8,128)(2,1)S(1)} %get-tuple-element.24), channel_id=1, source_target_pairs={{0,16},{2,18},{4,20},{6,22},{8,24},{10,26},{12,28},{14,30},{16,0},... | collective-permute-start | bytes 491528 | tf_op jit(solution)/shard_map/ppermute | solution.py:257
  7.1 1.3 %collective-permute-start.1 = (bf16[64,1280]{1,0:T(8,128)(2,1)S(1)}, bf16[64,1280]{1,0:T(8,128)(2,1)S(1)}, u32[]{:S(2)}, u32[]{:S(2)}) collective-permute-start(bf16[64,1280]{1,0:T(8,128)(2,1)S(1)} %get-tuple-element.25), channel_id=1, source_target_pairs={{0,20},{2,22},{4,16},{6,18},{8,28},{10,30},{12,24},{14,26},{16,4},... | collective-permute-start | bytes 491528 | tf_op jit(solution)/shard_map/ppermute | solution.py:257
  8.3 0.5 collective-permute-start.2
  8.9 3.6 %collective-permute-start.3 = (bf16[64,1280]{1,0:T(8,128)(2,1)S(1)}, bf16[64,1280]{1,0:T(8,128)(2,1)S(1)}, u32[]{:S(2)}, u32[]{:S(2)}) collective-permute-start(bf16[64,1280]{1,0:T(8,128)(2,1)S(1)} %get-tuple-element.29), channel_id=1, source_target_pairs={{0,24},{2,26},{4,28},{6,30},{8,16},{10,18},{12,20},{14,22},{16,8},... | collective-permute-start | bytes 491528 | tf_op jit(solution)/shard_map/ppermute | solution.py:257
  12.5 0.7 reshape.51.refs_4_
  13.2 0.7 reshape.52.refs_6_
  13.9 0.7 reshape.53.refs_7_
  14.6 0.2 compare_convert_fusion.refs_8_.refs_9_.refs_5_.refs_7_
  14.8 8.0 %collective-permute-done.refs_0_ = bf16[64,1280]{1,0:T(8,128)(2,1)S(1)} collective-permute-done((bf16[64,1280]{1,0:T(8,128)(2,1)S(1)}, bf16[64,1280]{1,0:T(8,128)(2,1)S(1)}, u32[]{:S(2)}, u32[]{:S(2)}) %collective-permute-start) | collective-permute-done | bytes 163872 | tf_op jit(solution)/shard_map/ppermute | solution.py:257
  22.7 3.3 %collective-permute-start.4 = (bf16[64,1280]{1,0:T(8,128)(2,1)S(1)}, bf16[64,1280]{1,0:T(8,128)(2,1)S(1)}, u32[]{:S(2)}, u32[]{:S(2)}) collective-permute-start(bf16[64,1280]{1,0:T(8,128)(2,1)S(1)} %get-tuple-element.30), channel_id=1, source_target_pairs={{0,28},{2,30},{4,24},{6,26},{8,20},{10,22},{12,16},{14,18},{16,12}... | collective-permute-start | bytes 491528 | tf_op jit(solution)/shard_map/ppermute | solution.py:257
  26.1 2.8 %collective-permute-done.1.refs_1_ = bf16[64,1280]{1,0:T(8,128)(2,1)S(1)} collective-permute-done((bf16[64,1280]{1,0:T(8,128)(2,1)S(1)}, bf16[64,1280]{1,0:T(8,128)(2,1)S(1)}, u32[]{:S(2)}, u32[]{:S(2)}) %collective-permute-start.1) | collective-permute-done | bytes 163872 | tf_op jit(solution)/shard_map/ppermute | solution.py:257
  28.9 0.0 collective-permute-start.5
  28.9 2.0 %collective-permute-start.6 = (bf16[64,1280]{1,0:T(8,128)(2,1)S(1)}, bf16[64,1280]{1,0:T(8,128)(2,1)S(1)}, u32[]{:S(2)}, u32[]{:S(2)}) collective-permute-start(bf16[64,1280]{1,0:T(8,128)(2,1)S(1)} %get-tuple-element.32), channel_id=1, source_target_pairs={{0,12},{2,14},{4,8},{6,10},{8,4},{10,6},{12,0},{14,2},{16,28},{18,... | collective-permute-start | bytes 491528 | tf_op jit(solution)/shard_map/ppermute | solution.py:257
  30.9 2.4 %copy-done.3 = bf16[1280,1920]{1,0:T(8,128)(2,1)S(1)} copy-done((bf16[1280,1920]{1,0:T(8,128)(2,1)S(1)}, bf16[1280,1920]{1,0:T(8,128)(2,1)}, u32[]{:S(2)}) %copy-start.3) | copy-done | bytes 4915224
  33.3 2.5 %time_first.1 = (bf16[4,64,640]{2,1,0:T(8,128)(2,1)S(1)}, bf16[2,4,64,640]{3,2,1,0:T(8,128)(2,1)S(1)}) custom-call(bf16[64,1280]{1,0:T(8,128)(2,1)S(1)} %collective-permute-done.refs_0_, bf16[64,1280]{1,0:T(8,128)(2,1)S(1)} %collective-permute-done.1.refs_1_, bf16[64,1280]{1,0:T(8,128)(2,1)S(1)} %get-tuple-element.26.refs_2_, ...), custom_call_target="tpu_custom_call" | custom-call | flops 2516582400 | bytes 1048576 | tf_op jit(solution)/shard_map/time_first/pallas_call | solution.py:207
  35.8 1.7 %collective-permute-done.6.refs_3_ = bf16[64,1280]{1,0:T(8,128)(2,1)S(1)} collective-permute-done((bf16[64,1280]{1,0:T(8,128)(2,1)S(1)}, bf16[64,1280]{1,0:T(8,128)(2,1)S(1)}, u32[]{:S(2)}, u32[]{:S(2)}) %collective-permute-start.6) | collective-permute-done | bytes 163872 | tf_op jit(solution)/shard_map/ppermute | solution.py:257
  37.6 2.5 %time_second.1 = (bf16[4,64,640]{2,1,0:T(8,128)(2,1)S(1)}, bf16[2,4,64,640]{3,2,1,0:T(8,128)(2,1)S(1)}) custom-call(bf16[64,1280]{1,0:T(8,128)(2,1)S(1)} %collective-permute-done.3.refs_0_, bf16[64,1280]{1,0:T(8,128)(2,1)S(1)} %collective-permute-done.4.refs_1_, bf16[64,1280]{1,0:T(8,128)(2,1)S(1)} %collective-permute-done.5.refs_2_, ...), custom_call_target="tpu_custom_call" | custom-call | flops 2516582400 | bytes 1048576 | tf_op jit(solution)/shard_map/time_second/pallas_call | solution.py:207
  40.1 0.1 collective-permute-start.8
  40.2 0.5 collective-permute-start.7
  40.7 1.5 %collective-permute-done.8.refs_5_ = bf16[2,4,64,640]{3,2,1,0:T(8,128)(2,1)S(1)} collective-permute-done((bf16[2,4,64,640]{3,2,1,0:T(8,128)(2,1)S(1)}, bf16[2,4,64,640]{3,2,1,0:T(8,128)(2,1)S(1)}, u32[]{:S(2)}, u32[]{:S(2)}) %collective-permute-start.8) | collective-permute-done | bytes 655392 | tf_op jit(solution)/shard_map/ppermute | solution.py:261
  42.3 0.9 %collective-permute-done.7.refs_3_ = bf16[2,4,64,640]{3,2,1,0:T(8,128)(2,1)S(1)} collective-permute-done((bf16[2,4,64,640]{3,2,1,0:T(8,128)(2,1)S(1)}, bf16[2,4,64,640]{3,2,1,0:T(8,128)(2,1)S(1)}, u32[]{:S(2)}, u32[]{:S(2)}) %collective-permute-start.7) | collective-permute-done | bytes 655392 | tf_op jit(solution)/shard_map/ppermute | solution.py:261
  43.2 1.8 %time_attention.1 = (bf16[2,64,640]{2,1,0:T(8,128)(2,1)S(1)}, bf16[2,64,640]{2,1,0:T(8,128)(2,1)S(1)}, bf16[2,64,640]{2,1,0:T(8,128)(2,1)S(1)}, bf16[2,64,640]{2,1,0:T(8,128)(2,1)S(1)}) custom-call(bf16[4,64,640]{2,1,0:T(8,128)(2,1)S(1)} %get-tuple-element.28.refs_9_.refs_0_, bf16[4,64,640]{2,1,0:T(8,128)(2,1)S(1)} %get-tuple-element.33.refs_1_, ...), custom_call_target="tpu_custom_call" | custom-call | flops 2516582400 | bytes 1048576 | tf_op jit(solution)/shard_map/time_attention/pallas_call | solution.py:207
  45.0 0.0 copy-start.2
  45.1 1.0 %collective-permute-start.14 = (bf16[64,640]{1,0:T(8,128)(2,1)S(1)}, bf16[64,640]{1,0:T(8,128)(2,1)S(1)}, u32[]{:S(2)}, u32[]{:S(2)}) collective-permute-start(bf16[64,640]{1,0:T(8,128)(2,1)S(1)} %relay.5), channel_id=1, source_target_pairs={{0,4},{2,6},{4,0},{6,2},{8,12},{10,14},{12,8},{14,10},{16,20},{18,... | collective-permute-start | bytes 245768 | tf_op jit(solution)/shard_map/ppermute | solution.py:299
  46.1 2.6 %collective-permute-start.11 = (bf16[2,64,640]{2,1,0:T(8,128)(2,1)S(1)}, bf16[2,64,640]{2,1,0:T(8,128)(2,1)S(1)}, u32[]{:S(2)}, u32[]{:S(2)}) collective-permute-start(bf16[2,64,640]{2,1,0:T(8,128)(2,1)S(1)} %get-tuple-element.37), channel_id=1, source_target_pairs={{0,8},{2,10},{4,12},{6,14},{8,0},{10,2},{12,4},{14,6},{16,24},{18,... | collective-permute-start | bytes 491528 | tf_op jit(solution)/shard_map/ppermute | solution.py:299
  48.7 2.0 %collective-permute-start.18 = (bf16[2,64,640]{2,1,0:T(8,128)(2,1)S(1)}, bf16[2,64,640]{2,1,0:T(8,128)(2,1)S(1)}, u32[]{:S(2)}, u32[]{:S(2)}) collective-permute-start(bf16[2,64,640]{2,1,0:T(8,128)(2,1)S(1)} %get-tuple-element.42), channel_id=1, source_target_pairs={{0,16},{2,18},{4,20},{6,22},{8,24},{10,26},{12,28},{14,30},{16,0},... | collective-permute-start | bytes 491528 | tf_op jit(solution)/shard_map/ppermute | solution.py:299
  50.7 1.5 %collective-permute-start.10 = (bf16[2,64,640]{2,1,0:T(8,128)(2,1)S(1)}, bf16[2,64,640]{2,1,0:T(8,128)(2,1)S(1)}, u32[]{:S(2)}, u32[]{:S(2)}) collective-permute-start(bf16[2,64,640]{2,1,0:T(8,128)(2,1)S(1)} %get-tuple-element.36), channel_id=1, source_target_pairs={{0,24},{2,26},{4,28},{6,30},{8,16},{10,18},{12,20},{14,22},{16,8},... | collective-permute-start | bytes 491528 | tf_op jit(solution)/shard_map/ppermute | solution.py:299
  52.2 0.6 collective-permute-start.15
  52.8 2.8 %collective-permute-done.11.landed_ref = bf16[2,64,640]{2,1,0:T(8,128)(2,1)S(1)} collective-permute-done((bf16[2,64,640]{2,1,0:T(8,128)(2,1)S(1)}, bf16[2,64,640]{2,1,0:T(8,128)(2,1)S(1)}, u32[]{:S(2)}, u32[]{:S(2)}) %collective-permute-start.11) | collective-permute-done | bytes 163872 | tf_op jit(solution)/shard_map/ppermute | solution.py:299
  55.6 1.3 %collective-permute-start.12 = (bf16[64,640]{1,0:T(8,128)(2,1)S(1)}, bf16[64,640]{1,0:T(8,128)(2,1)S(1)}, u32[]{:S(2)}, u32[]{:S(2)}) collective-permute-start(bf16[64,640]{1,0:T(8,128)(2,1)S(1)} %relay.4), channel_id=1, source_target_pairs={{0,4},{2,6},{4,0},{6,2},{8,12},{10,14},{12,8},{14,10},{16,20},{18,... | collective-permute-start | bytes 245768 | tf_op jit(solution)/shard_map/ppermute | solution.py:299
  57.0 3.2 %collective-permute-done.12.refs_1_ = bf16[64,640]{1,0:T(8,128)(2,1)S(1)} collective-permute-done((bf16[64,640]{1,0:T(8,128)(2,1)S(1)}, bf16[64,640]{1,0:T(8,128)(2,1)S(1)}, u32[]{:S(2)}, u32[]{:S(2)}) %collective-permute-start.12) | collective-permute-done | bytes 81952 | tf_op jit(solution)/shard_map/ppermute | solution.py:299
  60.2 0.6 collective-permute-start.13
  60.8 2.9 %space_clip.3.refs_10_.refs_11_ = bf16[128,640]{1,0:T(8,128)(2,1)S(1)} custom-call(bf16[128,640]{1,0:T(8,128)(2,1)S(1)} %gather.5.refs_0_, bf16[128,640]{1,0:T(8,128)(2,1)S(1)} %collective-permute-done.15.refs_1_, bf16[512,1280]{1,0:T(8,128)(2,1)S(1)} %bitcast.16, bf16[512,1280]{1,0:T(8,128)(2,1)S(1)} %collective-permute-done.9.refs_6_.refs_3_.refs_1_, ...), custom_call_target="tpu_custom_call" | custom-call | flops 2516582400 | bytes 1048576 | tf_op jit(solution)/shard_map/space_clip/pallas_call | solution.py:207
  63.7 1.8 %collective-permute-done.13.refs_1_ = bf16[128,640]{1,0:T(8,128)(2,1)S(1)} collective-permute-done((bf16[128,640]{1,0:T(8,128)(2,1)S(1)}, bf16[128,640]{1,0:T(8,128)(2,1)S(1)}, u32[]{:S(2)}, u32[]{:S(2)}) %collective-permute-start.13) | collective-permute-done | bytes 163872 | tf_op jit(solution)/shard_map/ppermute | solution.py:199
  65.6 3.1 %space_clip.4.refs_0_.refs_10_.refs_12_ = bf16[128,640]{1,0:T(8,128)(2,1)S(1)} custom-call(bf16[128,640]{1,0:T(8,128)(2,1)S(1)} %gather.4.refs_0_, bf16[128,640]{1,0:T(8,128)(2,1)S(1)} %collective-permute-done.13.refs_1_, bf16[512,1280]{1,0:T(8,128)(2,1)S(1)} %bitcast.17, bf16[512,1280]{1,0:T(8,128)(2,1)S(1)} %collective-permute-done.9.refs_6_.refs_3_.refs_1_, ...), custom_call_target="tpu_custom_call" | custom-call | flops 2516582400 | bytes 1048576 | tf_op jit(solution)/shard_map/space_clip/pallas_call | solution.py:207
  68.7 1.3 %collective-permute-start.19 = (bf16[64,640]{1,0:T(8,128)(2,1)S(1)}, bf16[64,640]{1,0:T(8,128)(2,1)S(1)}, u32[]{:S(2)}, u32[]{:S(2)}) collective-permute-start(bf16[64,640]{1,0:T(8,128)(2,1)S(1)} %relay.7), channel_id=1, source_target_pairs={{0,4},{2,6},{4,0},{6,2},{8,12},{10,14},{12,8},{14,10},{16,20},{18,... | collective-permute-start | bytes 245768 | tf_op jit(solution)/shard_map/ppermute | solution.py:299
  70.1 0.8 collective-permute-start.16
  70.9 2.3 %collective-permute-done.19.refs_1_ = bf16[64,640]{1,0:T(8,128)(2,1)S(1)} collective-permute-done((bf16[64,640]{1,0:T(8,128)(2,1)S(1)}, bf16[64,640]{1,0:T(8,128)(2,1)S(1)}, u32[]{:S(2)}, u32[]{:S(2)}) %collective-permute-start.19) | collective-permute-done | bytes 81952 | tf_op jit(solution)/shard_map/ppermute | solution.py:299
  73.3 0.6 collective-permute-start.20
  73.8 0.7 collective-permute-done.16.refs_1_
  74.6 0.9 %collective-permute-start.17 = (bf16[128,640]{1,0:T(8,128)(2,1)S(1)}, bf16[128,640]{1,0:T(8,128)(2,1)S(1)}, u32[]{:S(2)}, u32[]{:S(2)}) collective-permute-start(bf16[128,640]{1,0:T(8,128)(2,1)S(1)} %gather.6.block_ref), channel_id=1, source_target_pairs={{0,1},{1,0},{2,3},{3,2},{4,5},{5,4},{6,7},{7,6},{8,9},{9,8},{10,11... | collective-permute-start | bytes 491528 | tf_op jit(solution)/shard_map/ppermute | solution.py:199
  75.5 1.9 %space_own.1 = (bf16[128,640]{1,0:T(8,128)(2,1)S(1)}, bf16[128,640]{1,0:T(8,128)(2,1)S(1)}, bf16[128,640]{1,0:T(8,128)(2,1)S(1)}) custom-call(bf16[128,640]{1,0:T(8,128)(2,1)S(1)} %gather.6.block_ref, bf16[512,1280]{1,0:T(8,128)(2,1)S(1)} %bitcast.18, bf16[640,1280]{1,0:T(8,128)(2,1)S(1)} %copy-done, f32[1,1280]{1,0:T(1,128)S(1)} %reshape.54.refs_5_.refs_1_.refs_3_, ...), custom_call_target="tpu_custom_call" | custom-call | flops 1258291200 | bytes 1048576 | tf_op jit(solution)/shard_map/space_own/pallas_call | solution.py:207
  77.4 1.2 %collective-permute-done.20.refs_1_ = bf16[128,640]{1,0:T(8,128)(2,1)S(1)} collective-permute-done((bf16[128,640]{1,0:T(8,128)(2,1)S(1)}, bf16[128,640]{1,0:T(8,128)(2,1)S(1)}, u32[]{:S(2)}, u32[]{:S(2)}) %collective-permute-start.20) | collective-permute-done | bytes 163872 | tf_op jit(solution)/shard_map/ppermute | solution.py:199
  78.6 2.9 %space_clip.5.refs_13_ = bf16[128,640]{1,0:T(8,128)(2,1)S(1)} custom-call(bf16[128,640]{1,0:T(8,128)(2,1)S(1)} %gather.7.refs_0_, bf16[128,640]{1,0:T(8,128)(2,1)S(1)} %collective-permute-done.20.refs_1_, bf16[512,1280]{1,0:T(8,128)(2,1)S(1)} %bitcast.19, bf16[512,1280]{1,0:T(8,128)(2,1)S(1)} %collective-permute-done.9.refs_6_.refs_3_.refs_1_, ...), custom_call_target="tpu_custom_call" | custom-call | flops 2516582400 | bytes 1048576 | tf_op jit(solution)/shard_map/space_clip/pallas_call | solution.py:207
  81.5 2.7 %space_last.1 = bf16[4,128,640]{2,1,0:T(8,128)(2,1)} custom-call(bf16[128,640]{1,0:T(8,128)(2,1)S(1)} %collective-permute-done.17.refs_0_, bf16[512,1280]{1,0:T(8,128)(2,1)S(1)} %collective-permute-done.9.refs_6_.refs_3_.refs_1_, bf16[640,1280]{1,0:T(8,128)(2,1)S(1)} %copy-done, f32[1,1280]{1,0:T(1,128)S(1)} %reshape.54.refs_5_.refs_1_.refs_3_, ...), custom_call_target="tpu_custom_call" | custom-call | flops 1258291200 | bytes 1048576 | tf_op jit(solution)/shard_map/space_last/pallas_call | solution.py:207
  (42 shorter events, 0.3 us)
Async XLA Ops:
  0.0 43.2 %collective-permute-start.9 = (bf16[512,1280]{1,0:T(8,128)(2,1)}, bf16[512,1280]{1,0:T(8,128)(2,1)S(1)}, u32[]{:S(2)}, u32[]{:S(2)}) collective-permute-start(bf16[512,1280]{1,0:T(8,128)(2,1)} %bitcast.14), channel_id=1, source_target_pairs={{0,1},{1,0},{2,3},{3,2},{4,5},{5,4},{6,7},{7,6},{8,9},{9,8},{10,11... | collective-permute-start | bytes 3932168 | tf_op jit(solution)/shard_map/ppermute | solution.py:199
  3.0 1.4 %copy-start.1 = (bf16[4,1,128,1280]{3,2,1,0:T(8,128)(2,1)S(1)}, bf16[4,1,128,1280]{3,2,1,0:T(8,128)(2,1)}, u32[]{:S(2)}) copy-start(bf16[4,1,128,1280]{3,2,1,0:T(8,128)(2,1)} %param.10) | copy-start | bytes 3932164
  4.4 18.3 %collective-permute-start = (bf16[64,1280]{1,0:T(8,128)(2,1)S(1)}, bf16[64,1280]{1,0:T(8,128)(2,1)S(1)}, u32[]{:S(2)}, u32[]{:S(2)}) collective-permute-start(bf16[64,1280]{1,0:T(8,128)(2,1)S(1)} %get-tuple-element.24), channel_id=1, source_target_pairs={{0,16},{2,18},{4,20},{6,22},{8,24},{10,26},{12,28},{14,30},{16,0},... | collective-permute-start | bytes 491528 | tf_op jit(solution)/shard_map/ppermute | solution.py:257
  7.1 21.9 %collective-permute-start.1 = (bf16[64,1280]{1,0:T(8,128)(2,1)S(1)}, bf16[64,1280]{1,0:T(8,128)(2,1)S(1)}, u32[]{:S(2)}, u32[]{:S(2)}) collective-permute-start(bf16[64,1280]{1,0:T(8,128)(2,1)S(1)} %get-tuple-element.25), channel_id=1, source_target_pairs={{0,20},{2,22},{4,16},{6,18},{8,28},{10,30},{12,24},{14,26},{16,4},... | collective-permute-start | bytes 491528 | tf_op jit(solution)/shard_map/ppermute | solution.py:257
  8.3 20.6 %collective-permute-start.2 = (bf16[64,1280]{1,0:T(8,128)(2,1)S(1)}, bf16[64,1280]{1,0:T(8,128)(2,1)S(1)}, u32[]{:S(2)}, u32[]{:S(2)}) collective-permute-start(bf16[64,1280]{1,0:T(8,128)(2,1)S(1)} %get-tuple-element.27), channel_id=1, source_target_pairs={{0,4},{2,6},{4,0},{6,2},{8,12},{10,14},{12,8},{14,10},{16,20},{18,... | collective-permute-start | bytes 491528 | tf_op jit(solution)/shard_map/ppermute | solution.py:257
  8.9 27.0 %collective-permute-start.3 = (bf16[64,1280]{1,0:T(8,128)(2,1)S(1)}, bf16[64,1280]{1,0:T(8,128)(2,1)S(1)}, u32[]{:S(2)}, u32[]{:S(2)}) collective-permute-start(bf16[64,1280]{1,0:T(8,128)(2,1)S(1)} %get-tuple-element.29), channel_id=1, source_target_pairs={{0,24},{2,26},{4,28},{6,30},{8,16},{10,18},{12,20},{14,22},{16,8},... | collective-permute-start | bytes 491528 | tf_op jit(solution)/shard_map/ppermute | solution.py:257
  22.7 13.1 %collective-permute-start.4 = (bf16[64,1280]{1,0:T(8,128)(2,1)S(1)}, bf16[64,1280]{1,0:T(8,128)(2,1)S(1)}, u32[]{:S(2)}, u32[]{:S(2)}) collective-permute-start(bf16[64,1280]{1,0:T(8,128)(2,1)S(1)} %get-tuple-element.30), channel_id=1, source_target_pairs={{0,28},{2,30},{4,24},{6,26},{8,20},{10,22},{12,16},{14,18},{16,12}... | collective-permute-start | bytes 491528 | tf_op jit(solution)/shard_map/ppermute | solution.py:257
  28.9 6.9 %collective-permute-start.5 = (bf16[64,1280]{1,0:T(8,128)(2,1)S(1)}, bf16[64,1280]{1,0:T(8,128)(2,1)S(1)}, u32[]{:S(2)}, u32[]{:S(2)}) collective-permute-start(bf16[64,1280]{1,0:T(8,128)(2,1)S(1)} %get-tuple-element.31), channel_id=1, source_target_pairs={{0,8},{2,10},{4,12},{6,14},{8,0},{10,2},{12,4},{14,6},{16,24},{18,... | collective-permute-start | bytes 491528 | tf_op jit(solution)/shard_map/ppermute | solution.py:257
  28.9 8.7 %collective-permute-start.6 = (bf16[64,1280]{1,0:T(8,128)(2,1)S(1)}, bf16[64,1280]{1,0:T(8,128)(2,1)S(1)}, u32[]{:S(2)}, u32[]{:S(2)}) collective-permute-start(bf16[64,1280]{1,0:T(8,128)(2,1)S(1)} %get-tuple-element.32), channel_id=1, source_target_pairs={{0,12},{2,14},{4,8},{6,10},{8,4},{10,6},{12,0},{14,2},{16,28},{18,... | collective-permute-start | bytes 491528 | tf_op jit(solution)/shard_map/ppermute | solution.py:257
  30.9 2.4 %copy-start.3 = (bf16[1280,1920]{1,0:T(8,128)(2,1)S(1)}, bf16[1280,1920]{1,0:T(8,128)(2,1)}, u32[]{:S(2)}) copy-start(bf16[1280,1920]{1,0:T(8,128)(2,1)} %refs_5_.3) | copy-start | bytes 14745604
  37.6 3.1 %copy-start.4 = (f32[1280]{0:T(1024)S(1)}, f32[1280]{0:T(1024)}, u32[]{:S(2)}) copy-start(f32[1280]{0:T(1024)} %param.16) | copy-start | bytes 15364
  37.6 3.1 %copy-start.5 = (f32[640]{0:T(1024)S(1)}, f32[640]{0:T(1024)}, u32[]{:S(2)}) copy-start(f32[640]{0:T(1024)} %param.18) | copy-start | bytes 7684
  37.6 3.1 %copy-start.6 = (f32[640]{0:T(1024)S(1)}, f32[640]{0:T(1024)}, u32[]{:S(2)}) copy-start(f32[640]{0:T(1024)} %param.19) | copy-start | bytes 7684
  40.1 2.2 %collective-permute-start.8 = (bf16[2,4,64,640]{3,2,1,0:T(8,128)(2,1)S(1)}, bf16[2,4,64,640]{3,2,1,0:T(8,128)(2,1)S(1)}, u32[]{:S(2)}, u32[]{:S(2)}) collective-permute-start(bf16[2,4,64,640]{3,2,1,0:T(8,128)(2,1)S(1)} %get-tuple-element.35.refs_4_), channel_id=1, source_target_pairs={{0,2},{2,0},{4,6},{6,4},{8,10},{10,8},{12,14},{14,12},{16,18},{18,... | collective-permute-start | bytes 1966088 | tf_op jit(solution)/shard_map/ppermute | solution.py:261
  40.2 3.0 %collective-permute-start.7 = (bf16[2,4,64,640]{3,2,1,0:T(8,128)(2,1)S(1)}, bf16[2,4,64,640]{3,2,1,0:T(8,128)(2,1)S(1)}, u32[]{:S(2)}, u32[]{:S(2)}) collective-permute-start(bf16[2,4,64,640]{3,2,1,0:T(8,128)(2,1)S(1)} %get-tuple-element.34.refs_2_), channel_id=1, source_target_pairs={{0,2},{2,0},{4,6},{6,4},{8,10},{10,8},{12,14},{14,12},{16,18},{18,... | collective-permute-start | bytes 1966088 | tf_op jit(solution)/shard_map/ppermute | solution.py:261
  43.2 17.6 %slice-start = ((s8[4915200]{0:T(1024)(128)(4,1)}), s8[4194304]{0:T(1024)(128)(4,1)S(1)}, s32[]{:S(2)}) async-start(s8[4915200]{0:T(1024)(128)(4,1)} %bitcast.12), calls=%async_computation | async-start | bytes 8388608
  43.2 17.6 %slice-start.1 = ((s8[4915200]{0:T(1024)(128)(4,1)}), s8[720896]{0:T(1024)(128)(4,1)S(1)}, s32[]{:S(2)}) async-start(s8[4915200]{0:T(1024)(128)(4,1)} %bitcast.12), calls=%async_computation.1 | async-start | bytes 1441792
  43.2 17.6 %copy-start = (bf16[640,1280]{1,0:T(8,128)(2,1)S(1)}, bf16[640,1280]{1,0:T(8,128)(2,1)}, u32[]{:S(2)}) copy-start(bf16[640,1280]{1,0:T(8,128)(2,1)} %refs_2_.3) | copy-start | bytes 4915204
  45.0 15.7 %copy-start.2 = (bf16[4,1,128,1280]{3,2,1,0:T(8,128)(2,1)S(1)}, bf16[4,1,128,1280]{3,2,1,0:T(8,128)(2,1)}, u32[]{:S(2)}) copy-start(bf16[4,1,128,1280]{3,2,1,0:T(8,128)(2,1)} %param.10) | copy-start | bytes 3932164
  45.1 7.1 %collective-permute-start.14 = (bf16[64,640]{1,0:T(8,128)(2,1)S(1)}, bf16[64,640]{1,0:T(8,128)(2,1)S(1)}, u32[]{:S(2)}, u32[]{:S(2)}) collective-permute-start(bf16[64,640]{1,0:T(8,128)(2,1)S(1)} %relay.5), channel_id=1, source_target_pairs={{0,4},{2,6},{4,0},{6,2},{8,12},{10,14},{12,8},{14,10},{16,20},{18,... | collective-permute-start | bytes 245768 | tf_op jit(solution)/shard_map/ppermute | solution.py:299
  46.1 9.5 %collective-permute-start.11 = (bf16[2,64,640]{2,1,0:T(8,128)(2,1)S(1)}, bf16[2,64,640]{2,1,0:T(8,128)(2,1)S(1)}, u32[]{:S(2)}, u32[]{:S(2)}) collective-permute-start(bf16[2,64,640]{2,1,0:T(8,128)(2,1)S(1)} %get-tuple-element.37), channel_id=1, source_target_pairs={{0,8},{2,10},{4,12},{6,14},{8,0},{10,2},{12,4},{14,6},{16,24},{18,... | collective-permute-start | bytes 491528 | tf_op jit(solution)/shard_map/ppermute | solution.py:299
  48.7 20.0 %collective-permute-start.18 = (bf16[2,64,640]{2,1,0:T(8,128)(2,1)S(1)}, bf16[2,64,640]{2,1,0:T(8,128)(2,1)S(1)}, u32[]{:S(2)}, u32[]{:S(2)}) collective-permute-start(bf16[2,64,640]{2,1,0:T(8,128)(2,1)S(1)} %get-tuple-element.42), channel_id=1, source_target_pairs={{0,16},{2,18},{4,20},{6,22},{8,24},{10,26},{12,28},{14,30},{16,0},... | collective-permute-start | bytes 491528 | tf_op jit(solution)/shard_map/ppermute | solution.py:299
  50.7 19.4 %collective-permute-start.10 = (bf16[2,64,640]{2,1,0:T(8,128)(2,1)S(1)}, bf16[2,64,640]{2,1,0:T(8,128)(2,1)S(1)}, u32[]{:S(2)}, u32[]{:S(2)}) collective-permute-start(bf16[2,64,640]{2,1,0:T(8,128)(2,1)S(1)} %get-tuple-element.36), channel_id=1, source_target_pairs={{0,24},{2,26},{4,28},{6,30},{8,16},{10,18},{12,20},{14,22},{16,8},... | collective-permute-start | bytes 491528 | tf_op jit(solution)/shard_map/ppermute | solution.py:299
  52.2 8.5 %collective-permute-start.15 = (bf16[128,640]{1,0:T(8,128)(2,1)S(1)}, bf16[128,640]{1,0:T(8,128)(2,1)S(1)}, u32[]{:S(2)}, u32[]{:S(2)}) collective-permute-start(bf16[128,640]{1,0:T(8,128)(2,1)S(1)} %gather.5.refs_0_), channel_id=1, source_target_pairs={{0,1},{1,0},{2,3},{3,2},{4,5},{5,4},{6,7},{7,6},{8,9},{9,8},{10,11... | collective-permute-start | bytes 491528 | tf_op jit(solution)/shard_map/ppermute | solution.py:199
  55.6 4.5 %collective-permute-start.12 = (bf16[64,640]{1,0:T(8,128)(2,1)S(1)}, bf16[64,640]{1,0:T(8,128)(2,1)S(1)}, u32[]{:S(2)}, u32[]{:S(2)}) collective-permute-start(bf16[64,640]{1,0:T(8,128)(2,1)S(1)} %relay.4), channel_id=1, source_target_pairs={{0,4},{2,6},{4,0},{6,2},{8,12},{10,14},{12,8},{14,10},{16,20},{18,... | collective-permute-start | bytes 245768 | tf_op jit(solution)/shard_map/ppermute | solution.py:299
  60.2 5.4 %collective-permute-start.13 = (bf16[128,640]{1,0:T(8,128)(2,1)S(1)}, bf16[128,640]{1,0:T(8,128)(2,1)S(1)}, u32[]{:S(2)}, u32[]{:S(2)}) collective-permute-start(bf16[128,640]{1,0:T(8,128)(2,1)S(1)} %gather.4.refs_0_), channel_id=1, source_target_pairs={{0,1},{1,0},{2,3},{3,2},{4,5},{5,4},{6,7},{7,6},{8,9},{9,8},{10,11... | collective-permute-start | bytes 491528 | tf_op jit(solution)/shard_map/ppermute | solution.py:199
  68.7 4.5 %collective-permute-start.19 = (bf16[64,640]{1,0:T(8,128)(2,1)S(1)}, bf16[64,640]{1,0:T(8,128)(2,1)S(1)}, u32[]{:S(2)}, u32[]{:S(2)}) collective-permute-start(bf16[64,640]{1,0:T(8,128)(2,1)S(1)} %relay.7), channel_id=1, source_target_pairs={{0,4},{2,6},{4,0},{6,2},{8,12},{10,14},{12,8},{14,10},{16,20},{18,... | collective-permute-start | bytes 245768 | tf_op jit(solution)/shard_map/ppermute | solution.py:299
  70.1 4.5 %collective-permute-start.16 = (bf16[64,640]{1,0:T(8,128)(2,1)S(1)}, bf16[64,640]{1,0:T(8,128)(2,1)S(1)}, u32[]{:S(2)}, u32[]{:S(2)}) collective-permute-start(bf16[64,640]{1,0:T(8,128)(2,1)S(1)} %relay.6), channel_id=1, source_target_pairs={{0,4},{2,6},{4,0},{6,2},{8,12},{10,14},{12,8},{14,10},{16,20},{18,... | collective-permute-start | bytes 245768 | tf_op jit(solution)/shard_map/ppermute | solution.py:299
  73.3 5.4 %collective-permute-start.20 = (bf16[128,640]{1,0:T(8,128)(2,1)S(1)}, bf16[128,640]{1,0:T(8,128)(2,1)S(1)}, u32[]{:S(2)}, u32[]{:S(2)}) collective-permute-start(bf16[128,640]{1,0:T(8,128)(2,1)S(1)} %gather.7.refs_0_), channel_id=1, source_target_pairs={{0,1},{1,0},{2,3},{3,2},{4,5},{5,4},{6,7},{7,6},{8,9},{9,8},{10,11... | collective-permute-start | bytes 491528 | tf_op jit(solution)/shard_map/ppermute | solution.py:199
  74.6 6.9 %collective-permute-start.17 = (bf16[128,640]{1,0:T(8,128)(2,1)S(1)}, bf16[128,640]{1,0:T(8,128)(2,1)S(1)}, u32[]{:S(2)}, u32[]{:S(2)}) collective-permute-start(bf16[128,640]{1,0:T(8,128)(2,1)S(1)} %gather.6.block_ref), channel_id=1, source_target_pairs={{0,1},{1,0},{2,3},{3,2},{4,5},{5,4},{6,7},{7,6},{8,9},{9,8},{10,11... | collective-permute-start | bytes 491528 | tf_op jit(solution)/shard_map/ppermute | solution.py:199

commit v3 on v2

--- a/solution.py
+++ b/solution.py
@@ -24,9 +24,20 @@
     return (centred * lax.rsqrt(variance + EPS) * norm_gain).astype(jnp.bfloat16)
 
 
-def head_norm(part, gain, ones):
-    sums = jnp.dot((part * part).astype(jnp.bfloat16), ones, preferred_element_type=jnp.float32)
-    return (part * lax.rsqrt(sums * (1.0 / HDIM) + EPS) * gain).astype(jnp.bfloat16)
+def head_norm(part, gain, heads):
+    sums = lax.dot_general(
+        (part * part).astype(jnp.bfloat16),
+        heads[:LANES],
+        (((1,), (1,)), ((), ())),
+        preferred_element_type=jnp.float32,
+    )
+    inverse = lax.rsqrt(sums * (1.0 / HDIM) + EPS)
+    high = inverse.astype(jnp.bfloat16)
+    low = (inverse - high.astype(jnp.float32)).astype(jnp.bfloat16)
+    scale = jnp.dot(
+        jnp.concatenate([high, low], axis=1), heads, preferred_element_type=jnp.float32
+    )
+    return (part * scale * gain).astype(jnp.bfloat16)
 
 
 def lanes_of(head, tile, rows):
@@ -83,14 +94,14 @@
 
 def time_kernel(count, *refs):
     pieces, weights, (q_ref, kv_ref) = refs[:count], refs[count : count + 5], refs[-2:]
-    norm_ref, w_ref, qg_ref, kg_ref, ones_ref = weights
+    norm_ref, w_ref, qg_ref, kg_ref, heads_ref = weights
     inner = w_ref.shape[1] // 3
     normed = jnp.concatenate(
         [layer_norm(ref[...].astype(jnp.float32), norm_ref[...]) for ref in pieces], axis=0
     )
     product = jnp.dot(normed, w_ref[...], preferred_element_type=jnp.float32)
-    query = head_norm(product[:, :inner], qg_ref[...], ones_ref[...])
-    keys = head_norm(product[:, inner : 2 * inner], kg_ref[...], ones_ref[...])
+    query = head_norm(product[:, :inner], qg_ref[...], heads_ref[...])
+    keys = head_norm(product[:, inner : 2 * inner], kg_ref[...], heads_ref[...])
     shape = q_ref.shape
     q_ref[...] = query.reshape(shape)
     kv_ref[0] = keys.reshape(shape)
@@ -138,7 +149,7 @@
 
 
 def space_rows(blocks, clips, where, with_query, weights):
-    wo_ref, norm_ref, w_ref, qg_ref, kg_ref, ones_ref = weights
+    wo_ref, norm_ref, w_ref, qg_ref, kg_ref, heads_ref = weights
     patches, inner = blocks[0].shape
     at = pl.ds(pl.multiple_of(where * patches, patches), patches)
     normed = []
@@ -150,10 +161,10 @@
     query = None
     if with_query:
         product = jnp.dot(normed[0], w_ref[:, :inner], preferred_element_type=jnp.float32)
-        query = head_norm(product, qg_ref[...], ones_ref[...])
+        query = head_norm(product, qg_ref[...], heads_ref[...])
     normed = jnp.concatenate(normed, axis=0)
     product = jnp.dot(normed, w_ref[:, inner:], preferred_element_type=jnp.float32)
-    keys = head_norm(product[:, :inner], kg_ref[...], ones_ref[...])
+    keys = head_norm(product[:, :inner], kg_ref[...], heads_ref[...])
     return query, keys, product[:, inner:].astype(jnp.bfloat16)
 
 
@@ -239,11 +250,11 @@
     half = chips // 2
     count = chips // clips
     bf16 = jnp.bfloat16
-    head = jnp.arange(inner) // HDIM
-    ones = (head[:, None] == head[None, :]).astype(bf16)
+    lane = jnp.arange(2 * LANES) % LANES
+    heads = (lane[:, None] == jnp.arange(inner)[None, :] // HDIM).astype(bf16)
     quarter = max(1, half // 2)
     parts = [
-        list(range(half, half + quarter)) + list(range(quarter)),
+        list(range(quarter)) + list(range(half, half + quarter)),
         list(range(half + quarter, chips)) + list(range(quarter, half)),
     ]
     order = list(range(clips))
@@ -272,7 +283,7 @@
         w_time_qkv,
         q_gain_time.reshape(1, -1),
         k_gain_time.reshape(1, -1),
-        ones,
+        heads,
     ]
     queries, held = [], []
     for members, name in zip(parts, ("time_first", "time_second")):
@@ -305,7 +316,7 @@
         w_space_qkv,
         q_gain_space.reshape(1, -1),
         k_gain_space.reshape(1, -1),
-        ones,
+        heads,
     ]
     room = 24 + 8 * (sides - 2)
     block_shape = (patches, inner)

time: 84.5 us -> 85.1 us (level)
  starting transfers between devices: 30.1 us -> 26.6 us
  waiting for transfers between devices: 27.2 us -> 30.7 us
    ppermute x7, starting transfers between devices: 13.4 us -> 9.27 us  [exchange(): moved[k] = lax.ppermute(pieces[k], 'frame', pairs)]
    ppermute x7, waiting for transfers between devices: 12.6 us -> 16.3 us  [exchange(): moved[k] = lax.ppermute(pieces[k], 'frame', pairs)]
    unnamed x18 -> x20, local copies, waits for them, and re-layouts: 3.77 us -> 3.78 us
where the time goes in v3:
time: 85.1 us; the launch traced here: 84.8 us
  waiting for transfers between devices  30.7 us (36%)
  starting transfers between devices  26.6 us (31%)
  Pallas kernels  21.1 us (25%)
  local copies, waits for them, and re-layouts  5.9 us (7%)
    pallas_call x17, Pallas kernels, call(): pl.pallas_call(kernel, out_shape=shapes, in_specs=[VMEM] * (len(operands)...  21.1 us
    ppermute x7, waiting for transfers between devices, exchange(): moved[k] = lax.ppermute(pieces[k], 'frame', pairs)  16.3 us
    ppermute x7, starting transfers between devices, step_to(): return lax.ppermute(array, 'frame', [(i, i ^ 2 * k) for i in range(frames)])  11.4 us
    ppermute x7, starting transfers between devices, exchange(): moved[k] = lax.ppermute(pieces[k], 'frame', pairs)  9.27 us
    ppermute x7, waiting for transfers between devices, step_to(): return lax.ppermute(array, 'frame', [(i, i ^ 2 * k) for i in range(frames)])  9.1 us
    ppermute x5, starting transfers between devices, from_sides(): lax.ppermute(array, 'patch', [(i, (i - hop) % size) for i in range(size)])  5.34 us
    unnamed x20, local copies, waits for them, and re-layouts  3.78 us
    ppermute x5, waiting for transfers between devices, from_sides(): lax.ppermute(array, 'patch', [(i, (i - hop) % size) for i in range(size)])  2.92 us
  transfers between devices with their start and end apart: 21, of which 11 were waited for; matrix products, arithmetic and copies ran while one was open for 3% of the time, Pallas kernels for 19%

profile of v3, /device:TPU:0, one launch (start us, length us, event | category | flops | bytes accessed | tf_op | source)
XLA Modules:
  0.0 84.8 jit_solution(15448910173195784448)
XLA Ops:
  0.0 3.0 %collective-permute-start.9 = (bf16[512,1280]{1,0:T(8,128)(2,1)}, bf16[512,1280]{1,0:T(8,128)(2,1)S(1)}, u32[]{:S(2)}, u32[]{:S(2)}) collective-permute-start(bf16[512,1280]{1,0:T(8,128)(2,1)} %bitcast.14), channel_id=1, source_target_pairs={{0,1},{1,0},{2,3},{3,2},{4,5},{5,4},{6,7},{7,6},{8,9},{9,8},{10,11... | collective-permute-start | bytes 3932168 | tf_op jit(solution)/shard_map/ppermute | solution.py:210
  3.0 1.3 %copy-done.1 = bf16[4,1,128,1280]{3,2,1,0:T(8,128)(2,1)S(1)} copy-done((bf16[4,1,128,1280]{3,2,1,0:T(8,128)(2,1)S(1)}, bf16[4,1,128,1280]{3,2,1,0:T(8,128)(2,1)}, u32[]{:S(2)}) %copy-start.1) | copy-done | bytes 1310744
  4.3 0.1 pack.1
  4.4 1.6 %collective-permute-start = (bf16[64,1280]{1,0:T(8,128)(2,1)S(1)}, bf16[64,1280]{1,0:T(8,128)(2,1)S(1)}, u32[]{:S(2)}, u32[]{:S(2)}) collective-permute-start(bf16[64,1280]{1,0:T(8,128)(2,1)S(1)} %get-tuple-element.25), channel_id=1, source_target_pairs={{0,4},{2,6},{4,0},{6,2},{8,12},{10,14},{12,8},{14,10},{16,20},{18,... | collective-permute-start | bytes 491528 | tf_op jit(solution)/shard_map/ppermute | solution.py:268
  6.0 2.6 %collective-permute-start.1 = (bf16[64,1280]{1,0:T(8,128)(2,1)S(1)}, bf16[64,1280]{1,0:T(8,128)(2,1)S(1)}, u32[]{:S(2)}, u32[]{:S(2)}) collective-permute-start(bf16[64,1280]{1,0:T(8,128)(2,1)S(1)} %get-tuple-element.26), channel_id=1, source_target_pairs={{0,16},{2,18},{4,20},{6,22},{8,24},{10,26},{12,28},{14,30},{16,0},... | collective-permute-start | bytes 491528 | tf_op jit(solution)/shard_map/ppermute | solution.py:268
  8.6 0.3 collective-permute-start.2
  8.9 3.6 %collective-permute-start.3 = (bf16[64,1280]{1,0:T(8,128)(2,1)S(1)}, bf16[64,1280]{1,0:T(8,128)(2,1)S(1)}, u32[]{:S(2)}, u32[]{:S(2)}) collective-permute-start(bf16[64,1280]{1,0:T(8,128)(2,1)S(1)} %get-tuple-element.29), channel_id=1, source_target_pairs={{0,24},{2,26},{4,28},{6,30},{8,16},{10,18},{12,20},{14,22},{16,8},... | collective-permute-start | bytes 491528 | tf_op jit(solution)/shard_map/ppermute | solution.py:268
  12.5 0.7 reshape.57.refs_4_
  13.2 0.7 reshape.58.refs_6_
  13.9 0.7 reshape.59.refs_7_
  14.6 0.1 compare_convert_fusion.refs_8_.refs_9_.refs_5_.refs_7_
  14.7 1.2 %collective-permute-start.4 = (bf16[64,1280]{1,0:T(8,128)(2,1)S(1)}, bf16[64,1280]{1,0:T(8,128)(2,1)S(1)}, u32[]{:S(2)}, u32[]{:S(2)}) collective-permute-start(bf16[64,1280]{1,0:T(8,128)(2,1)S(1)} %get-tuple-element.30), channel_id=1, source_target_pairs={{0,28},{2,30},{4,24},{6,26},{8,20},{10,22},{12,16},{14,18},{16,12}... | collective-permute-start | bytes 491528 | tf_op jit(solution)/shard_map/ppermute | solution.py:268
  15.9 11.5 %collective-permute-done.1.refs_2_ = bf16[64,1280]{1,0:T(8,128)(2,1)S(1)} collective-permute-done((bf16[64,1280]{1,0:T(8,128)(2,1)S(1)}, bf16[64,1280]{1,0:T(8,128)(2,1)S(1)}, u32[]{:S(2)}, u32[]{:S(2)}) %collective-permute-start.1) | collective-permute-done | bytes 163872 | tf_op jit(solution)/shard_map/ppermute | solution.py:268
  27.5 0.0 collective-permute-start.5
  27.5 3.5 %collective-permute-done.2.refs_3_ = bf16[64,1280]{1,0:T(8,128)(2,1)S(1)} collective-permute-done((bf16[64,1280]{1,0:T(8,128)(2,1)S(1)}, bf16[64,1280]{1,0:T(8,128)(2,1)S(1)}, u32[]{:S(2)}, u32[]{:S(2)}) %collective-permute-start.2) | collective-permute-done | bytes 163872 | tf_op jit(solution)/shard_map/ppermute | solution.py:268
  30.9 0.0 collective-permute-start.6
  30.9 2.4 %copy-done.3 = bf16[1280,1920]{1,0:T(8,128)(2,1)S(1)} copy-done((bf16[1280,1920]{1,0:T(8,128)(2,1)S(1)}, bf16[1280,1920]{1,0:T(8,128)(2,1)}, u32[]{:S(2)}) %copy-start.3) | copy-done | bytes 4915224
  33.3 2.6 %time_first.1 = (bf16[4,64,640]{2,1,0:T(8,128)(2,1)S(1)}, bf16[2,4,64,640]{3,2,1,0:T(8,128)(2,1)S(1)}) custom-call(bf16[64,1280]{1,0:T(8,128)(2,1)S(1)} %get-tuple-element.24.refs_0_, bf16[64,1280]{1,0:T(8,128)(2,1)S(1)} %collective-permute-done.refs_1_, bf16[64,1280]{1,0:T(8,128)(2,1)S(1)} %collective-permute-done.1.refs_2_, ...), custom_call_target="tpu_custom_call" | custom-call | flops 2516582400 | bytes 1048576 | tf_op jit(solution)/shard_map/time_first/pallas_call | solution.py:218
  35.9 1.2 %collective-permute-done.6.refs_3_ = bf16[64,1280]{1,0:T(8,128)(2,1)S(1)} collective-permute-done((bf16[64,1280]{1,0:T(8,128)(2,1)S(1)}, bf16[64,1280]{1,0:T(8,128)(2,1)S(1)}, u32[]{:S(2)}, u32[]{:S(2)}) %collective-permute-start.6) | collective-permute-done | bytes 163872 | tf_op jit(solution)/shard_map/ppermute | solution.py:268
  37.2 2.6 %time_second.1 = (bf16[4,64,640]{2,1,0:T(8,128)(2,1)S(1)}, bf16[2,4,64,640]{3,2,1,0:T(8,128)(2,1)S(1)}) custom-call(bf16[64,1280]{1,0:T(8,128)(2,1)S(1)} %collective-permute-done.3.refs_0_, bf16[64,1280]{1,0:T(8,128)(2,1)S(1)} %collective-permute-done.4.refs_1_, bf16[64,1280]{1,0:T(8,128)(2,1)S(1)} %collective-permute-done.5.refs_2_, ...), custom_call_target="tpu_custom_call" | custom-call | flops 2516582400 | bytes 1048576 | tf_op jit(solution)/shard_map/time_second/pallas_call | solution.py:218
  39.8 0.1 collective-permute-start.8
  39.9 0.5 collective-permute-start.7
  40.4 1.5 %collective-permute-done.8.refs_5_ = bf16[2,4,64,640]{3,2,1,0:T(8,128)(2,1)S(1)} collective-permute-done((bf16[2,4,64,640]{3,2,1,0:T(8,128)(2,1)S(1)}, bf16[2,4,64,640]{3,2,1,0:T(8,128)(2,1)S(1)}, u32[]{:S(2)}, u32[]{:S(2)}) %collective-permute-start.8) | collective-permute-done | bytes 655392 | tf_op jit(solution)/shard_map/ppermute | solution.py:272
  42.0 0.9 %collective-permute-done.7.refs_3_ = bf16[2,4,64,640]{3,2,1,0:T(8,128)(2,1)S(1)} collective-permute-done((bf16[2,4,64,640]{3,2,1,0:T(8,128)(2,1)S(1)}, bf16[2,4,64,640]{3,2,1,0:T(8,128)(2,1)S(1)}, u32[]{:S(2)}, u32[]{:S(2)}) %collective-permute-start.7) | collective-permute-done | bytes 655392 | tf_op jit(solution)/shard_map/ppermute | solution.py:272
  42.9 1.8 %time_attention.1 = (bf16[2,64,640]{2,1,0:T(8,128)(2,1)S(1)}, bf16[2,64,640]{2,1,0:T(8,128)(2,1)S(1)}, bf16[2,64,640]{2,1,0:T(8,128)(2,1)S(1)}, bf16[2,64,640]{2,1,0:T(8,128)(2,1)S(1)}) custom-call(bf16[4,64,640]{2,1,0:T(8,128)(2,1)S(1)} %get-tuple-element.28.refs_9_.refs_0_, bf16[4,64,640]{2,1,0:T(8,128)(2,1)S(1)} %get-tuple-element.33.refs_1_, ...), custom_call_target="tpu_custom_call" | custom-call | flops 2516582400 | bytes 1048576 | tf_op jit(solution)/shard_map/time_attention/pallas_call | solution.py:218
  44.7 0.0 copy-start.2
  44.8 1.6 %collective-permute-start.14 = (bf16[64,640]{1,0:T(8,128)(2,1)S(1)}, bf16[64,640]{1,0:T(8,128)(2,1)S(1)}, u32[]{:S(2)}, u32[]{:S(2)}) collective-permute-start(bf16[64,640]{1,0:T(8,128)(2,1)S(1)} %relay.5), channel_id=1, source_target_pairs={{0,4},{2,6},{4,0},{6,2},{8,12},{10,14},{12,8},{14,10},{16,20},{18,... | collective-permute-start | bytes 245768 | tf_op jit(solution)/shard_map/ppermute | solution.py:310
  46.3 2.8 %collective-permute-start.11 = (bf16[2,64,640]{2,1,0:T(8,128)(2,1)S(1)}, bf16[2,64,640]{2,1,0:T(8,128)(2,1)S(1)}, u32[]{:S(2)}, u32[]{:S(2)}) collective-permute-start(bf16[2,64,640]{2,1,0:T(8,128)(2,1)S(1)} %get-tuple-element.37), channel_id=1, source_target_pairs={{0,8},{2,10},{4,12},{6,14},{8,0},{10,2},{12,4},{14,6},{16,24},{18,... | collective-permute-start | bytes 491528 | tf_op jit(solution)/shard_map/ppermute | solution.py:310
  49.1 1.9 %collective-permute-start.18 = (bf16[2,64,640]{2,1,0:T(8,128)(2,1)S(1)}, bf16[2,64,640]{2,1,0:T(8,128)(2,1)S(1)}, u32[]{:S(2)}, u32[]{:S(2)}) collective-permute-start(bf16[2,64,640]{2,1,0:T(8,128)(2,1)S(1)} %get-tuple-element.42), channel_id=1, source_target_pairs={{0,16},{2,18},{4,20},{6,22},{8,24},{10,26},{12,28},{14,30},{16,0},... | collective-permute-start | bytes 491528 | tf_op jit(solution)/shard_map/ppermute | solution.py:310
  51.0 1.5 %collective-permute-start.10 = (bf16[2,64,640]{2,1,0:T(8,128)(2,1)S(1)}, bf16[2,64,640]{2,1,0:T(8,128)(2,1)S(1)}, u32[]{:S(2)}, u32[]{:S(2)}) collective-permute-start(bf16[2,64,640]{2,1,0:T(8,128)(2,1)S(1)} %get-tuple-element.36), channel_id=1, source_target_pairs={{0,24},{2,26},{4,28},{6,30},{8,16},{10,18},{12,20},{14,22},{16,8},... | collective-permute-start | bytes 491528 | tf_op jit(solution)/shard_map/ppermute | solution.py:310
  52.6 0.6 collective-permute-start.15
  53.1 2.9 %collective-permute-done.11.landed_ref = bf16[2,64,640]{2,1,0:T(8,128)(2,1)S(1)} collective-permute-done((bf16[2,64,640]{2,1,0:T(8,128)(2,1)S(1)}, bf16[2,64,640]{2,1,0:T(8,128)(2,1)S(1)}, u32[]{:S(2)}, u32[]{:S(2)}) %collective-permute-start.11) | collective-permute-done | bytes 163872 | tf_op jit(solution)/shard_map/ppermute | solution.py:310
  56.0 1.5 %collective-permute-start.12 = (bf16[64,640]{1,0:T(8,128)(2,1)S(1)}, bf16[64,640]{1,0:T(8,128)(2,1)S(1)}, u32[]{:S(2)}, u32[]{:S(2)}) collective-permute-start(bf16[64,640]{1,0:T(8,128)(2,1)S(1)} %relay.4), channel_id=1, source_target_pairs={{0,4},{2,6},{4,0},{6,2},{8,12},{10,14},{12,8},{14,10},{16,20},{18,... | collective-permute-start | bytes 245768 | tf_op jit(solution)/shard_map/ppermute | solution.py:310
  57.5 3.0 %collective-permute-done.12.refs_1_ = bf16[64,640]{1,0:T(8,128)(2,1)S(1)} collective-permute-done((bf16[64,640]{1,0:T(8,128)(2,1)S(1)}, bf16[64,640]{1,0:T(8,128)(2,1)S(1)}, u32[]{:S(2)}, u32[]{:S(2)}) %collective-permute-start.12) | collective-permute-done | bytes 81952 | tf_op jit(solution)/shard_map/ppermute | solution.py:310
  60.6 0.6 collective-permute-start.13
  61.2 3.0 %space_clip.3.refs_10_.refs_11_ = bf16[128,640]{1,0:T(8,128)(2,1)S(1)} custom-call(bf16[128,640]{1,0:T(8,128)(2,1)S(1)} %gather.5.refs_0_, bf16[128,640]{1,0:T(8,128)(2,1)S(1)} %collective-permute-done.15.refs_1_, bf16[512,1280]{1,0:T(8,128)(2,1)S(1)} %bitcast.16, bf16[512,1280]{1,0:T(8,128)(2,1)S(1)} %collective-permute-done.9.refs_6_.refs_3_.refs_1_, ...), custom_call_target="tpu_custom_call" | custom-call | flops 2516582400 | bytes 1048576 | tf_op jit(solution)/shard_map/space_clip/pallas_call | solution.py:218
  64.1 1.8 %collective-permute-done.13.refs_1_ = bf16[128,640]{1,0:T(8,128)(2,1)S(1)} collective-permute-done((bf16[128,640]{1,0:T(8,128)(2,1)S(1)}, bf16[128,640]{1,0:T(8,128)(2,1)S(1)}, u32[]{:S(2)}, u32[]{:S(2)}) %collective-permute-start.13) | collective-permute-done | bytes 163872 | tf_op jit(solution)/shard_map/ppermute | solution.py:210
  65.9 3.1 %space_clip.4.refs_0_.refs_10_.refs_12_ = bf16[128,640]{1,0:T(8,128)(2,1)S(1)} custom-call(bf16[128,640]{1,0:T(8,128)(2,1)S(1)} %gather.4.refs_0_, bf16[128,640]{1,0:T(8,128)(2,1)S(1)} %collective-permute-done.13.refs_1_, bf16[512,1280]{1,0:T(8,128)(2,1)S(1)} %bitcast.17, bf16[512,1280]{1,0:T(8,128)(2,1)S(1)} %collective-permute-done.9.refs_6_.refs_3_.refs_1_, ...), custom_call_target="tpu_custom_call" | custom-call | flops 2516582400 | bytes 1048576 | tf_op jit(solution)/shard_map/space_clip/pallas_call | solution.py:218
  69.1 1.5 %collective-permute-start.19 = (bf16[64,640]{1,0:T(8,128)(2,1)S(1)}, bf16[64,640]{1,0:T(8,128)(2,1)S(1)}, u32[]{:S(2)}, u32[]{:S(2)}) collective-permute-start(bf16[64,640]{1,0:T(8,128)(2,1)S(1)} %relay.7), channel_id=1, source_target_pairs={{0,4},{2,6},{4,0},{6,2},{8,12},{10,14},{12,8},{14,10},{16,20},{18,... | collective-permute-start | bytes 245768 | tf_op jit(solution)/shard_map/ppermute | solution.py:310
  70.7 0.6 collective-permute-start.16
  71.3 2.3 %collective-permute-done.19.refs_1_ = bf16[64,640]{1,0:T(8,128)(2,1)S(1)} collective-permute-done((bf16[64,640]{1,0:T(8,128)(2,1)S(1)}, bf16[64,640]{1,0:T(8,128)(2,1)S(1)}, u32[]{:S(2)}, u32[]{:S(2)}) %collective-permute-start.19) | collective-permute-done | bytes 81952 | tf_op jit(solution)/shard_map/ppermute | solution.py:310
  73.7 0.6 collective-permute-start.20
  74.2 0.9 %collective-permute-done.16.refs_1_ = bf16[64,640]{1,0:T(8,128)(2,1)S(1)} collective-permute-done((bf16[64,640]{1,0:T(8,128)(2,1)S(1)}, bf16[64,640]{1,0:T(8,128)(2,1)S(1)}, u32[]{:S(2)}, u32[]{:S(2)}) %collective-permute-start.16) | collective-permute-done | bytes 81952 | tf_op jit(solution)/shard_map/ppermute | solution.py:310
  75.2 0.7 collective-permute-start.17
  75.9 2.0 %space_own.1 = (bf16[128,640]{1,0:T(8,128)(2,1)S(1)}, bf16[128,640]{1,0:T(8,128)(2,1)S(1)}, bf16[128,640]{1,0:T(8,128)(2,1)S(1)}) custom-call(bf16[128,640]{1,0:T(8,128)(2,1)S(1)} %gather.6.block_ref, bf16[512,1280]{1,0:T(8,128)(2,1)S(1)} %bitcast.18, bf16[640,1280]{1,0:T(8,128)(2,1)S(1)} %copy-done, f32[1,1280]{1,0:T(1,128)S(1)} %reshape.60.refs_5_.refs_1_.refs_3_, ...), custom_call_target="tpu_custom_call" | custom-call | flops 1258291200 | bytes 1048576 | tf_op jit(solution)/shard_map/space_own/pallas_call | solution.py:218
  77.9 1.1 %collective-permute-done.20.refs_1_ = bf16[128,640]{1,0:T(8,128)(2,1)S(1)} collective-permute-done((bf16[128,640]{1,0:T(8,128)(2,1)S(1)}, bf16[128,640]{1,0:T(8,128)(2,1)S(1)}, u32[]{:S(2)}, u32[]{:S(2)}) %collective-permute-start.20) | collective-permute-done | bytes 163872 | tf_op jit(solution)/shard_map/ppermute | solution.py:210
  79.0 3.0 %space_clip.5.refs_13_ = bf16[128,640]{1,0:T(8,128)(2,1)S(1)} custom-call(bf16[128,640]{1,0:T(8,128)(2,1)S(1)} %gather.7.refs_0_, bf16[128,640]{1,0:T(8,128)(2,1)S(1)} %collective-permute-done.20.refs_1_, bf16[512,1280]{1,0:T(8,128)(2,1)S(1)} %bitcast.19, bf16[512,1280]{1,0:T(8,128)(2,1)S(1)} %collective-permute-done.9.refs_6_.refs_3_.refs_1_, ...), custom_call_target="tpu_custom_call" | custom-call | flops 2516582400 | bytes 1048576 | tf_op jit(solution)/shard_map/space_clip/pallas_call | solution.py:218
  82.0 2.8 %space_last.1 = bf16[4,128,640]{2,1,0:T(8,128)(2,1)} custom-call(bf16[128,640]{1,0:T(8,128)(2,1)S(1)} %collective-permute-done.17.refs_0_, bf16[512,1280]{1,0:T(8,128)(2,1)S(1)} %collective-permute-done.9.refs_6_.refs_3_.refs_1_, bf16[640,1280]{1,0:T(8,128)(2,1)S(1)} %copy-done, f32[1,1280]{1,0:T(1,128)S(1)} %reshape.60.refs_5_.refs_1_.refs_3_, ...), custom_call_target="tpu_custom_call" | custom-call | flops 1258291200 | bytes 1048576 | tf_op jit(solution)/shard_map/space_last/pallas_call | solution.py:218
  (45 shorter events, 0.3 us)
Async XLA Ops:
  0.0 42.9 %collective-permute-start.9 = (bf16[512,1280]{1,0:T(8,128)(2,1)}, bf16[512,1280]{1,0:T(8,128)(2,1)S(1)}, u32[]{:S(2)}, u32[]{:S(2)}) collective-permute-start(bf16[512,1280]{1,0:T(8,128)(2,1)} %bitcast.14), channel_id=1, source_target_pairs={{0,1},{1,0},{2,3},{3,2},{4,5},{5,4},{6,7},{7,6},{8,9},{9,8},{10,11... | collective-permute-start | bytes 3932168 | tf_op jit(solution)/shard_map/ppermute | solution.py:210
  3.0 1.4 %copy-start.1 = (bf16[4,1,128,1280]{3,2,1,0:T(8,128)(2,1)S(1)}, bf16[4,1,128,1280]{3,2,1,0:T(8,128)(2,1)}, u32[]{:S(2)}) copy-start(bf16[4,1,128,1280]{3,2,1,0:T(8,128)(2,1)} %param.10) | copy-start | bytes 3932164
  4.4 10.3 %collective-permute-start = (bf16[64,1280]{1,0:T(8,128)(2,1)S(1)}, bf16[64,1280]{1,0:T(8,128)(2,1)S(1)}, u32[]{:S(2)}, u32[]{:S(2)}) collective-permute-start(bf16[64,1280]{1,0:T(8,128)(2,1)S(1)} %get-tuple-element.25), channel_id=1, source_target_pairs={{0,4},{2,6},{4,0},{6,2},{8,12},{10,14},{12,8},{14,10},{16,20},{18,... | collective-permute-start | bytes 491528 | tf_op jit(solution)/shard_map/ppermute | solution.py:268
  6.0 21.5 %collective-permute-start.1 = (bf16[64,1280]{1,0:T(8,128)(2,1)S(1)}, bf16[64,1280]{1,0:T(8,128)(2,1)S(1)}, u32[]{:S(2)}, u32[]{:S(2)}) collective-permute-start(bf16[64,1280]{1,0:T(8,128)(2,1)S(1)} %get-tuple-element.26), channel_id=1, source_target_pairs={{0,16},{2,18},{4,20},{6,22},{8,24},{10,26},{12,28},{14,30},{16,0},... | collective-permute-start | bytes 491528 | tf_op jit(solution)/shard_map/ppermute | solution.py:268
  8.6 22.4 %collective-permute-start.2 = (bf16[64,1280]{1,0:T(8,128)(2,1)S(1)}, bf16[64,1280]{1,0:T(8,128)(2,1)S(1)}, u32[]{:S(2)}, u32[]{:S(2)}) collective-permute-start(bf16[64,1280]{1,0:T(8,128)(2,1)S(1)} %get-tuple-element.27), channel_id=1, source_target_pairs={{0,20},{2,22},{4,16},{6,18},{8,28},{10,30},{12,24},{14,26},{16,4},... | collective-permute-start | bytes 491528 | tf_op jit(solution)/shard_map/ppermute | solution.py:268
  8.9 27.1 %collective-permute-start.3 = (bf16[64,1280]{1,0:T(8,128)(2,1)S(1)}, bf16[64,1280]{1,0:T(8,128)(2,1)S(1)}, u32[]{:S(2)}, u32[]{:S(2)}) collective-permute-start(bf16[64,1280]{1,0:T(8,128)(2,1)S(1)} %get-tuple-element.29), channel_id=1, source_target_pairs={{0,24},{2,26},{4,28},{6,30},{8,16},{10,18},{12,20},{14,22},{16,8},... | collective-permute-start | bytes 491528 | tf_op jit(solution)/shard_map/ppermute | solution.py:268
  14.7 21.2 %collective-permute-start.4 = (bf16[64,1280]{1,0:T(8,128)(2,1)S(1)}, bf16[64,1280]{1,0:T(8,128)(2,1)S(1)}, u32[]{:S(2)}, u32[]{:S(2)}) collective-permute-start(bf16[64,1280]{1,0:T(8,128)(2,1)S(1)} %get-tuple-element.30), channel_id=1, source_target_pairs={{0,28},{2,30},{4,24},{6,26},{8,20},{10,22},{12,16},{14,18},{16,12}... | collective-permute-start | bytes 491528 | tf_op jit(solution)/shard_map/ppermute | solution.py:268
  27.5 8.5 %collective-permute-start.5 = (bf16[64,1280]{1,0:T(8,128)(2,1)S(1)}, bf16[64,1280]{1,0:T(8,128)(2,1)S(1)}, u32[]{:S(2)}, u32[]{:S(2)}) collective-permute-start(bf16[64,1280]{1,0:T(8,128)(2,1)S(1)} %get-tuple-element.31), channel_id=1, source_target_pairs={{0,8},{2,10},{4,12},{6,14},{8,0},{10,2},{12,4},{14,6},{16,24},{18,... | collective-permute-start | bytes 491528 | tf_op jit(solution)/shard_map/ppermute | solution.py:268
  30.9 6.2 %collective-permute-start.6 = (bf16[64,1280]{1,0:T(8,128)(2,1)S(1)}, bf16[64,1280]{1,0:T(8,128)(2,1)S(1)}, u32[]{:S(2)}, u32[]{:S(2)}) collective-permute-start(bf16[64,1280]{1,0:T(8,128)(2,1)S(1)} %get-tuple-element.32), channel_id=1, source_target_pairs={{0,12},{2,14},{4,8},{6,10},{8,4},{10,6},{12,0},{14,2},{16,28},{18,... | collective-permute-start | bytes 491528 | tf_op jit(solution)/shard_map/ppermute | solution.py:268
  30.9 2.4 %copy-start.3 = (bf16[1280,1920]{1,0:T(8,128)(2,1)S(1)}, bf16[1280,1920]{1,0:T(8,128)(2,1)}, u32[]{:S(2)}) copy-start(bf16[1280,1920]{1,0:T(8,128)(2,1)} %refs_5_.3) | copy-start | bytes 14745604
  33.3 3.8 %copy-start.4 = (bf16[1280,1920]{1,0:T(8,128)(2,1)S(1)}, bf16[1280,1920]{1,0:T(8,128)(2,1)}, u32[]{:S(2)}) copy-start(bf16[1280,1920]{1,0:T(8,128)(2,1)} %refs_5_.3) | copy-start | bytes 14745604
  37.2 3.2 %copy-start.5 = (f32[1280]{0:T(1024)S(1)}, f32[1280]{0:T(1024)}, u32[]{:S(2)}) copy-start(f32[1280]{0:T(1024)} %param.16) | copy-start | bytes 15364
  37.2 3.2 %copy-start.6 = (f32[640]{0:T(1024)S(1)}, f32[640]{0:T(1024)}, u32[]{:S(2)}) copy-start(f32[640]{0:T(1024)} %param.18) | copy-start | bytes 7684
  37.2 3.2 %copy-start.7 = (f32[640]{0:T(1024)S(1)}, f32[640]{0:T(1024)}, u32[]{:S(2)}) copy-start(f32[640]{0:T(1024)} %param.19) | copy-start | bytes 7684
  39.8 2.2 %collective-permute-start.8 = (bf16[2,4,64,640]{3,2,1,0:T(8,128)(2,1)S(1)}, bf16[2,4,64,640]{3,2,1,0:T(8,128)(2,1)S(1)}, u32[]{:S(2)}, u32[]{:S(2)}) collective-permute-start(bf16[2,4,64,640]{3,2,1,0:T(8,128)(2,1)S(1)} %get-tuple-element.35.refs_4_), channel_id=1, source_target_pairs={{0,2},{2,0},{4,6},{6,4},{8,10},{10,8},{12,14},{14,12},{16,18},{18,... | collective-permute-start | bytes 1966088 | tf_op jit(solution)/shard_map/ppermute | solution.py:272
  39.9 3.0 %collective-permute-start.7 = (bf16[2,4,64,640]{3,2,1,0:T(8,128)(2,1)S(1)}, bf16[2,4,64,640]{3,2,1,0:T(8,128)(2,1)S(1)}, u32[]{:S(2)}, u32[]{:S(2)}) collective-permute-start(bf16[2,4,64,640]{3,2,1,0:T(8,128)(2,1)S(1)} %get-tuple-element.34.refs_2_), channel_id=1, source_target_pairs={{0,2},{2,0},{4,6},{6,4},{8,10},{10,8},{12,14},{14,12},{16,18},{18,... | collective-permute-start | bytes 1966088 | tf_op jit(solution)/shard_map/ppermute | solution.py:272
  42.9 18.2 %slice-start = ((s8[4915200]{0:T(1024)(128)(4,1)}), s8[4194304]{0:T(1024)(128)(4,1)S(1)}, s32[]{:S(2)}) async-start(s8[4915200]{0:T(1024)(128)(4,1)} %bitcast.12), calls=%async_computation | async-start | bytes 8388608
  42.9 18.2 %slice-start.1 = ((s8[4915200]{0:T(1024)(128)(4,1)}), s8[720896]{0:T(1024)(128)(4,1)S(1)}, s32[]{:S(2)}) async-start(s8[4915200]{0:T(1024)(128)(4,1)} %bitcast.12), calls=%async_computation.1 | async-start | bytes 1441792
  42.9 18.2 %copy-start = (bf16[640,1280]{1,0:T(8,128)(2,1)S(1)}, bf16[640,1280]{1,0:T(8,128)(2,1)}, u32[]{:S(2)}) copy-start(bf16[640,1280]{1,0:T(8,128)(2,1)} %refs_2_.3) | copy-start | bytes 4915204
  44.7 16.4 %copy-start.2 = (bf16[4,1,128,1280]{3,2,1,0:T(8,128)(2,1)S(1)}, bf16[4,1,128,1280]{3,2,1,0:T(8,128)(2,1)}, u32[]{:S(2)}) copy-start(bf16[4,1,128,1280]{3,2,1,0:T(8,128)(2,1)} %param.10) | copy-start | bytes 3932164
  44.8 7.8 %collective-permute-start.14 = (bf16[64,640]{1,0:T(8,128)(2,1)S(1)}, bf16[64,640]{1,0:T(8,128)(2,1)S(1)}, u32[]{:S(2)}, u32[]{:S(2)}) collective-permute-start(bf16[64,640]{1,0:T(8,128)(2,1)S(1)} %relay.5), channel_id=1, source_target_pairs={{0,4},{2,6},{4,0},{6,2},{8,12},{10,14},{12,8},{14,10},{16,20},{18,... | collective-permute-start | bytes 245768 | tf_op jit(solution)/shard_map/ppermute | solution.py:310
  46.3 9.7 %collective-permute-start.11 = (bf16[2,64,640]{2,1,0:T(8,128)(2,1)S(1)}, bf16[2,64,640]{2,1,0:T(8,128)(2,1)S(1)}, u32[]{:S(2)}, u32[]{:S(2)}) collective-permute-start(bf16[2,64,640]{2,1,0:T(8,128)(2,1)S(1)} %get-tuple-element.37), channel_id=1, source_target_pairs={{0,8},{2,10},{4,12},{6,14},{8,0},{10,2},{12,4},{14,6},{16,24},{18,... | collective-permute-start | bytes 491528 | tf_op jit(solution)/shard_map/ppermute | solution.py:310
  49.1 20.0 %collective-permute-start.18 = (bf16[2,64,640]{2,1,0:T(8,128)(2,1)S(1)}, bf16[2,64,640]{2,1,0:T(8,128)(2,1)S(1)}, u32[]{:S(2)}, u32[]{:S(2)}) collective-permute-start(bf16[2,64,640]{2,1,0:T(8,128)(2,1)S(1)} %get-tuple-element.42), channel_id=1, source_target_pairs={{0,16},{2,18},{4,20},{6,22},{8,24},{10,26},{12,28},{14,30},{16,0},... | collective-permute-start | bytes 491528 | tf_op jit(solution)/shard_map/ppermute | solution.py:310
  51.0 19.7 %collective-permute-start.10 = (bf16[2,64,640]{2,1,0:T(8,128)(2,1)S(1)}, bf16[2,64,640]{2,1,0:T(8,128)(2,1)S(1)}, u32[]{:S(2)}, u32[]{:S(2)}) collective-permute-start(bf16[2,64,640]{2,1,0:T(8,128)(2,1)S(1)} %get-tuple-element.36), channel_id=1, source_target_pairs={{0,24},{2,26},{4,28},{6,30},{8,16},{10,18},{12,20},{14,22},{16,8},... | collective-permute-start | bytes 491528 | tf_op jit(solution)/shard_map/ppermute | solution.py:310
  52.6 8.6 %collective-permute-start.15 = (bf16[128,640]{1,0:T(8,128)(2,1)S(1)}, bf16[128,640]{1,0:T(8,128)(2,1)S(1)}, u32[]{:S(2)}, u32[]{:S(2)}) collective-permute-start(bf16[128,640]{1,0:T(8,128)(2,1)S(1)} %gather.5.refs_0_), channel_id=1, source_target_pairs={{0,1},{1,0},{2,3},{3,2},{4,5},{5,4},{6,7},{7,6},{8,9},{9,8},{10,11... | collective-permute-start | bytes 491528 | tf_op jit(solution)/shard_map/ppermute | solution.py:210
  56.0 4.5 %collective-permute-start.12 = (bf16[64,640]{1,0:T(8,128)(2,1)S(1)}, bf16[64,640]{1,0:T(8,128)(2,1)S(1)}, u32[]{:S(2)}, u32[]{:S(2)}) collective-permute-start(bf16[64,640]{1,0:T(8,128)(2,1)S(1)} %relay.4), channel_id=1, source_target_pairs={{0,4},{2,6},{4,0},{6,2},{8,12},{10,14},{12,8},{14,10},{16,20},{18,... | collective-permute-start | bytes 245768 | tf_op jit(solution)/shard_map/ppermute | solution.py:310
  60.6 5.4 %collective-permute-start.13 = (bf16[128,640]{1,0:T(8,128)(2,1)S(1)}, bf16[128,640]{1,0:T(8,128)(2,1)S(1)}, u32[]{:S(2)}, u32[]{:S(2)}) collective-permute-start(bf16[128,640]{1,0:T(8,128)(2,1)S(1)} %gather.4.refs_0_), channel_id=1, source_target_pairs={{0,1},{1,0},{2,3},{3,2},{4,5},{5,4},{6,7},{7,6},{8,9},{9,8},{10,11... | collective-permute-start | bytes 491528 | tf_op jit(solution)/shard_map/ppermute | solution.py:210
  69.1 4.5 %collective-permute-start.19 = (bf16[64,640]{1,0:T(8,128)(2,1)S(1)}, bf16[64,640]{1,0:T(8,128)(2,1)S(1)}, u32[]{:S(2)}, u32[]{:S(2)}) collective-permute-start(bf16[64,640]{1,0:T(8,128)(2,1)S(1)} %relay.7), channel_id=1, source_target_pairs={{0,4},{2,6},{4,0},{6,2},{8,12},{10,14},{12,8},{14,10},{16,20},{18,... | collective-permute-start | bytes 245768 | tf_op jit(solution)/shard_map/ppermute | solution.py:310
  70.7 4.5 %collective-permute-start.16 = (bf16[64,640]{1,0:T(8,128)(2,1)S(1)}, bf16[64,640]{1,0:T(8,128)(2,1)S(1)}, u32[]{:S(2)}, u32[]{:S(2)}) collective-permute-start(bf16[64,640]{1,0:T(8,128)(2,1)S(1)} %relay.6), channel_id=1, source_target_pairs={{0,4},{2,6},{4,0},{6,2},{8,12},{10,14},{12,8},{14,10},{16,20},{18,... | collective-permute-start | bytes 245768 | tf_op jit(solution)/shard_map/ppermute | solution.py:310
  73.7 5.4 %collective-permute-start.20 = (bf16[128,640]{1,0:T(8,128)(2,1)S(1)}, bf16[128,640]{1,0:T(8,128)(2,1)S(1)}, u32[]{:S(2)}, u32[]{:S(2)}) collective-permute-start(bf16[128,640]{1,0:T(8,128)(2,1)S(1)} %gather.7.refs_0_), channel_id=1, source_target_pairs={{0,1},{1,0},{2,3},{3,2},{4,5},{5,4},{6,7},{7,6},{8,9},{9,8},{10,11... | collective-permute-start | bytes 491528 | tf_op jit(solution)/shard_map/ppermute | solution.py:210
  75.2 6.8 %collective-permute-start.17 = (bf16[128,640]{1,0:T(8,128)(2,1)S(1)}, bf16[128,640]{1,0:T(8,128)(2,1)S(1)}, u32[]{:S(2)}, u32[]{:S(2)}) collective-permute-start(bf16[128,640]{1,0:T(8,128)(2,1)S(1)} %gather.6.block_ref), channel_id=1, source_target_pairs={{0,1},{1,0},{2,3},{3,2},{4,5},{5,4},{6,7},{7,6},{8,9},{9,8},{10,11... | collective-permute-start | bytes 491528 | tf_op jit(solution)/shard_map/ppermute | solution.py:210
